TPU v7x, 512 devices: a whole 4x4x16 slice. The times are simulated.
512 devices in a mesh: pole: 16 (over x, z_hi), leaf: 32 (over y, z_lo, core).
Axes of the slice: x: 4, y: 4, z: 16 (z_hi: 4, z_lo: 4; z = z_hi * 4 + z_lo), core: 2. Of those that a mesh axis runs over, the one named last changes fastest.
Arguments:
- root_inverse: bfloat16 [16, 2, 2048, 2048], P('pole', None, 'leaf'), may hold values from -6 to 6
- factor_child: bfloat16 [16, 2, 192, 4096], P('pole', None, None, 'leaf'), may hold values from -0.3125 to 0.3125
- factor_grand: bfloat16 [16, 2, 192, 8192], P('pole', None, None, 'leaf'), may hold values from -0.3125 to 0.3125
- diag_child: bfloat16 [16, 2, 2048, 4096], P('pole', None, None, 'leaf'), may hold values from -6 to 6
- diag_grand: bfloat16 [16, 2, 2048, 8192], P('pole', None, None, 'leaf'), may hold values from -6 to 6
- struct_child: int32 [2, 192], replicated, may hold values from 0 to 2047, as said below
- struct_grand: int32 [4, 192], replicated, may hold values from 0 to 2239, as said below
- pole_weight: float32 [16, 2], P('pole'), may hold values from -1.5 to 1.5
Outputs:
- density_child: float32 [2048, 4096], P('pole', 'leaf')
- density_grand: float32 [2048, 8192], P('pole', 'leaf')
Inputs may be any that keep to these rules, and one draw needn't show every extreme that they name: `struct_child`: each row holds 192 distinct increasing indices of the root separator's 2048 rows. `struct_grand`: each row holds 192 distinct increasing indices: the first half below 2048 (rows of the parent separator), the second half from 2048 on (the parent's structure rows).
All inputs are finite; a program needn't handle non-finite values.
Results may differ from a plain program's by a relative error of at most 0.004.
Values may be sent and summed in bfloat16 or wider, within the bound.
A program may use at most 64 MiB of HBM per device.

v0:
```python
import jax
import jax.numpy as jnp
from jax import lax
from jax.sharding import PartitionSpec as P


def partner_2(x, axis, distance):
    return lax.ppermute(x, axis, [(i, i ^ 1 << distance) for i in range(lax.axis_size(axis))])


def complex_left(ancestor):
    upper = jnp.concatenate([ancestor[0], -ancestor[1]], axis=1)
    bottom = jnp.concatenate([ancestor[1], ancestor[0]], axis=1)
    return jnp.concatenate([upper, bottom], axis=0)


def solve_block(ancestor, factor_cols, factor_all, diag_cols):
    rows_count = factor_cols.shape[1]
    breadth = factor_cols.shape[2]
    stacked = factor_cols.reshape(2 * rows_count, breadth)
    product = jnp.dot(complex_left(ancestor), stacked, preferred_element_type=jnp.float32)
    xblock = (-product).astype(jnp.bfloat16).reshape(2, rows_count, breadth)
    off_real = xblock[0]
    off_imag = xblock[1]
    right_block = jnp.concatenate(
        [
            jnp.concatenate([off_real, off_imag], axis=1),
            jnp.concatenate([-off_imag, off_real], axis=1),
        ],
        axis=0,
    )
    factor_flat = factor_all.reshape(2 * rows_count, factor_all.shape[2])
    reduced = lax.dot_general(
        factor_flat, right_block, (((0,), (0,)), ((), ())), preferred_element_type=jnp.float32
    )
    yblock = (
        diag_cols.astype(jnp.float32) - jnp.stack([reduced[:, :breadth], reduced[:, breadth:]])
    ).astype(jnp.bfloat16)
    return (xblock, yblock)


def density_term(inverse_block, weight_real, weight_imag):
    return weight_real * inverse_block[1].astype(jnp.float32) + weight_imag * inverse_block[
        0
    ].astype(jnp.float32)


def ordered_join(own_piece, partner, lower_half):
    first_part = jnp.where(lower_half, own_piece, partner)
    second_part = jnp.where(lower_half, partner, own_piece)
    return jnp.concatenate([first_part, second_part], axis=2)


def local(
    root_inverse,
    factor_child,
    factor_grand,
    diag_child,
    diag_grand,
    struct_child,
    struct_grand,
    pole_weight,
):
    leaf_count = lax.axis_size("leaf")
    device = lax.axis_index("leaf")
    levels = leaf_count.bit_length() - 1
    half_count = leaf_count // 2
    quarter_count = leaf_count // 4
    root_rows = root_inverse[0]
    row_count = root_rows.shape[1]
    order = root_rows.shape[2]
    rows_count = struct_child.shape[1]
    child_index = device // half_count
    within = device % half_count
    grand_local = device // quarter_count % 2
    weight_real = pole_weight[0, 0]
    weight_imag = pole_weight[0, 1]
    columns_taken = jnp.take(root_rows, struct_child, axis=2)
    row_ids = device * row_count + jnp.arange(row_count, dtype=jnp.int32)
    picker = (struct_child[:, :, None] == row_ids[None, None, :]).astype(jnp.bfloat16)
    pieces = jnp.einsum("ckj,rjcl->crkl", picker, columns_taken, preferred_element_type=jnp.float32)
    blocks = lax.psum(pieces.astype(jnp.bfloat16), "leaf").astype(jnp.float32)
    ancestor = lax.dynamic_index_in_dim(blocks, child_index, 0, keepdims=False).astype(jnp.bfloat16)
    child_cols = factor_child[0]
    child_all = child_cols
    for level_bit in range(levels - 1):
        partner = partner_2(child_all, "leaf", level_bit)
        lower_half = device // 2**level_bit % 2 == 0
        child_all = ordered_join(child_all, partner, lower_half)
    child_off, child_inverse = solve_block(ancestor, child_cols, child_all, diag_child[0])
    density_child_term = density_term(child_inverse, weight_real, weight_imag)
    density_child = lax.psum_scatter(density_child_term, "pole", scatter_dimension=0, tiled=True)
    breadth = child_off.shape[2]
    column_ids = within * breadth + jnp.arange(breadth, dtype=jnp.int32)
    chosen = lax.dynamic_slice_in_dim(struct_grand, 2 * child_index, 2, 0)
    owner_mask = (chosen[:, :, None] == column_ids[None, None, :]).astype(jnp.bfloat16)
    ext_cols = jnp.concatenate([child_inverse, child_off], axis=1)
    ext_rows = jnp.take(ext_cols, chosen, axis=1)
    column_terms = jnp.einsum(
        "rgkj,glj->grkl", ext_rows, owner_mask, preferred_element_type=jnp.float32
    )
    beyond = (chosen >= order).astype(jnp.float32)
    off_index = jnp.clip(chosen - order, 0, rows_count - 1)
    off_rows = jnp.take(child_off, off_index, axis=1)
    mirror_terms = (
        jnp.einsum("gkj,rglj->grkl", owner_mask, off_rows, preferred_element_type=jnp.float32)
        * beyond[:, None, None, :]
    )
    contributions = column_terms + mirror_terms
    summed = contributions
    for level_bit in range(levels - 1):
        summed = summed + partner_2(summed.astype(jnp.bfloat16), "leaf", level_bit).astype(
            jnp.float32
        )
    own_sum = lax.dynamic_index_in_dim(summed, grand_local, 0, keepdims=False)
    own_rows = lax.dynamic_index_in_dim(chosen, grand_local, 0, keepdims=False)
    interior = own_rows >= order
    local_index = jnp.clip(own_rows - order, 0, rows_count - 1)
    local_part = jnp.take(jnp.take(ancestor, local_index, axis=1), local_index, axis=2)
    local_part = jnp.where(
        interior[None, :, None] & interior[None, None, :], local_part, jnp.zeros_like(local_part)
    )
    ancestor_grand = (own_sum + local_part.astype(jnp.float32)).astype(jnp.bfloat16)
    grand_cols = factor_grand[0]
    grand_all = grand_cols
    for level_bit in range(levels - 2):
        partner = partner_2(grand_all, "leaf", level_bit)
        lower_half = device // 2**level_bit % 2 == 0
        grand_all = ordered_join(grand_all, partner, lower_half)
    grand_off, grand_inverse = solve_block(ancestor_grand, grand_cols, grand_all, diag_grand[0])
    density_grand_term = density_term(grand_inverse, weight_real, weight_imag)
    density_grand = lax.psum_scatter(density_grand_term, "pole", scatter_dimension=0, tiled=True)
    return (density_child, density_grand)


def solution(mesh):
    placed = (
        P("pole", None, "leaf", None),
        P("pole", None, None, "leaf"),
        P("pole", None, None, "leaf"),
        P("pole", None, None, "leaf"),
        P("pole", None, None, "leaf"),
        P(),
        P(),
        P("pole", None),
    )
    return jax.shard_map(
        local,
        mesh=mesh,
        in_specs=placed,
        out_specs=(P("pole", "leaf"), P("pole", "leaf")),
        check_vma=False,
    )
```

profile of v0, /device:TPU:1, one launch (start us, length us, event | category | flops | bytes accessed | tf_op | source)
XLA Modules:
  0.0 647.8 jit_solution(17774779574312855669)
XLA Ops:
  7.3 8.9 %collective-permute-start = (bf16[2,192,128]{2,1,0:T(8,128)(2,1)}, bf16[2,192,128]{2,1,0:T(8,128)(2,1)S(1)}, u32[]{:S(2)}, u32[]{:S(2)}) collective-permute-start(bf16[2,192,128]{2,1,0:T(8,128)(2,1)} %bitcast.102), channel_id=1, source_target_pairs={{0,1},{1,0},{2,3},{3,2},{4,5},{5,4},{6,7},{7,6},{8,9},{9,8},{10,11... | collective-permute-start | bytes 294920 | tf_op jit(solution)/shard_map/ppermute | solution.py:8
  16.2 1.9 collective-permute-start.4
  20.3 2.3 copy.37
  22.7 2.0 gather_fusion
  24.9 1.1 fusion.4
  27.2 1.9 collective-permute-start.1
  29.2 5.9 collective-permute-done.1
  35.2 1.9 collective-permute-start.2
  37.2 0.8 pad_maximum_fusion.6
  38.0 2.2 collective-permute-start.5
  40.2 259.8 %all-reduce.2.cloned.1.call-done = bf16[2,2,192,192]{2,3,1,0:T(8,128)(2,1)} async-done(((bf16[2,2,192,192]{2,3,1,0:T(8,128)(2,1)}), bf16[2,2,192,192]{2,3,1,0:T(8,128)(2,1)}) %all-reduce.2.cloned.1.call-update) | async-done | bytes 294928 | tf_op jit(solution)/shard_map/psum | solution.py:82
  300.0 0.9 convert_convert_fusion
  301.2 1.9 collective-permute-start.3
  303.7 2.4 gather_fusion.2
  306.0 12.6 %collective-permute-done.3 = bf16[2,192,1024]{2,1,0:T(8,128)(2,1)} collective-permute-done((bf16[2,192,1024]{2,1,0:T(8,128)(2,1)S(1)}, bf16[2,192,1024]{2,1,0:T(8,128)(2,1)}, u32[]{:S(2)}, u32[]{:S(2)}) %collective-permute-start.3) | collective-permute-done | bytes 786464 | tf_op jit(solution)/shard_map/ppermute | solution.py:8
  318.6 1.5 broadcast_select_fusion.3
  320.2 0.8 fusion.32
  321.2 1.1 copy-done.6
  322.6 9.9 %copy.39 = bf16[2,2240,128]{2,0,1:T(2,128)(2,1)S(1)} copy(bf16[2,2240,128]{2,1,0:T(8,128)(2,1)S(1)} %pad_maximum_fusion.2) | data formatting | bytes 2293760 | tf_op jit(solution)/shard_map/concatenate | solution.py:97
  332.5 2.0 gather_fusion.1
  334.9 1.3 fusion.77
  336.2 6.6 %collective-permute-start.7 = (bf16[2,2,192,192]{3,2,1,0:T(8,128)(2,1)S(1)}, bf16[2,2,192,192]{3,2,1,0:T(8,128)(2,1)S(1)}, u32[]{:S(2)}, u32[]{:S(2)}) collective-permute-start(bf16[2,2,192,192]{3,2,1,0:T(8,128)(2,1)S(1)} %get-tuple-element.41), channel_id=1, source_target_pairs={{0,1},{1,0},{2,3},{3,2},{4,5},{5,4},{6,7},{7,6},{8,9},{9,8},{10,11... | collective-permute-start | bytes 884744 | tf_op jit(solution)/shard_map/ppermute | solution.py:8
  342.8 1.1 broadcast_select_fusion.6
  343.9 1.0 pad_maximum_fusion.4
  344.9 1.9 collective-permute-start.6
  346.9 0.9 fusion.7
  347.8 1.9 collective-permute-start.8
  349.7 0.7 fusion.82
  350.4 1.8 copy.43
  352.2 2.7 gather_fusion.3
  354.9 1.9 fusion.43
  356.8 1.8 copy.44
  358.6 2.7 gather_fusion.4
  361.3 11.4 %collective-permute-done.8 = bf16[2,2,192,192]{3,2,1,0:T(8,128)(2,1)S(1)} collective-permute-done((bf16[2,2,192,192]{3,2,1,0:T(8,128)(2,1)}, bf16[2,2,192,192]{3,2,1,0:T(8,128)(2,1)S(1)}, u32[]{:S(2)}, u32[]{:S(2)}) %collective-permute-start.8) | collective-permute-done | bytes 294944 | tf_op jit(solution)/shard_map/ppermute | solution.py:8
  372.9 1.9 collective-permute-start.9
  374.8 14.9 %collective-permute-done.6 = bf16[2,192,1024]{2,1,0:T(8,128)(2,1)} collective-permute-done((bf16[2,192,1024]{2,1,0:T(8,128)(2,1)}, bf16[2,192,1024]{2,1,0:T(8,128)(2,1)}, u32[]{:S(2)}, u32[]{:S(2)}) %collective-permute-start.6) | collective-permute-done | bytes 786464 | tf_op jit(solution)/shard_map/ppermute | solution.py:8
  389.7 1.5 broadcast_select_fusion.1
  391.4 6.7 %collective-permute-done.9 = bf16[2,2,192,192]{3,2,1,0:T(8,128)(2,1)S(1)} collective-permute-done((bf16[2,2,192,192]{3,2,1,0:T(8,128)(2,1)S(1)}, bf16[2,2,192,192]{3,2,1,0:T(8,128)(2,1)S(1)}, u32[]{:S(2)}, u32[]{:S(2)}) %collective-permute-start.9) | collective-permute-done | bytes 294944 | tf_op jit(solution)/shard_map/ppermute | solution.py:8
  398.0 1.3 fusion.72
  399.3 2.0 collective-permute-start.10
  401.4 2.4 add_bitcast_fusion.1
  404.1 7.8 %collective-permute-done.10 = bf16[2,2,192,192]{3,2,1,0:T(8,128)(2,1)} collective-permute-done((bf16[2,2,192,192]{3,2,1,0:T(8,128)(2,1)}, bf16[2,2,192,192]{3,2,1,0:T(8,128)(2,1)}, u32[]{:S(2)}, u32[]{:S(2)}) %collective-permute-start.10) | collective-permute-done | bytes 294944 | tf_op jit(solution)/shard_map/ppermute | solution.py:8
  411.9 1.0 fusion.8
  414.5 1.3 fusion.9
  416.1 1.3 copy-done.2
  418.0 2.9 add_bitcast_fusion
  421.0 94.0 %reduce-scatter.3.cloned.1.call-done = f32[128,128]{1,0:T(8,128)} async-done(((f32[2048,128]{1,0:T(8,128)}), f32[128,128]{1,0:T(8,128)}) %reduce-scatter.3.cloned.1.call-update) | async-done | bytes 65552 | tf_op jit(solution)/shard_map/reduce_scatter | solution.py:92
  514.9 126.3 %reduce-scatter.5.cloned.1.call-done = f32[128,256]{1,0:T(8,128)} async-done(((f32[2048,256]{1,0:T(8,128)}), f32[128,256]{1,0:T(8,128)}) %reduce-scatter.5.cloned.1.call-update) | async-done | bytes 131088 | tf_op jit(solution)/shard_map/reduce_scatter | solution.py:132
  (86 shorter events, 8.3 us)
Async XLA Ops:
  7.2 20.0 %copy-start.11 = (bf16[1,2,192,128]{3,2,1,0:T(8,128)(2,1)S(1)}, bf16[1,2,192,128]{3,2,1,0:T(8,128)(2,1)}, u32[]{:S(2)}) copy-start(bf16[1,2,192,128]{3,2,1,0:T(8,128)(2,1)} %param.9) | copy-start | bytes 294916
  7.2 18.9 %copy-start.13 = (s32[4,192]{1,0:T(4,128)S(1)}, s32[4,192]{1,0:T(4,128)}, u32[]{:S(2)}) copy-start(s32[4,192]{1,0:T(4,128)} %param.14) | copy-start | bytes 9220
  7.2 17.7 %copy-start.12 = (s32[2,192]{1,0:T(2,128)S(1)}, s32[2,192]{1,0:T(2,128)}, u32[]{:S(2)}) copy-start(s32[2,192]{1,0:T(2,128)} %param.13) | copy-start | bytes 4612
  7.2 19.0 %copy-start.14 = (f32[1,2]{1,0:T(1,128)S(1)}, f32[1,2]{1,0:T(1,128)}, u32[]{:S(2)}) copy-start(f32[1,2]{1,0:T(1,128)} %param.15) | copy-start | bytes 28
  7.2 292.8 %all-reduce.2.cloned.1.call-start = ((), (), s32[]{:S(2)}) async-start(), calls=%async_computation.2 | async-start | bytes 786432 | tf_op jit(solution)/shard_map/psum | solution.py:82
  7.3 19.9 %collective-permute-start = (bf16[2,192,128]{2,1,0:T(8,128)(2,1)}, bf16[2,192,128]{2,1,0:T(8,128)(2,1)S(1)}, u32[]{:S(2)}, u32[]{:S(2)}) collective-permute-start(bf16[2,192,128]{2,1,0:T(8,128)(2,1)} %bitcast.102), channel_id=1, source_target_pairs={{0,1},{1,0},{2,3},{3,2},{4,5},{5,4},{6,7},{7,6},{8,9},{9,8},{10,11... | collective-permute-start | bytes 294920 | tf_op jit(solution)/shard_map/ppermute | solution.py:8
  16.2 21.0 %collective-permute-start.4 = (bf16[2,192,256]{2,1,0:T(8,128)(2,1)}, bf16[2,192,256]{2,1,0:T(8,128)(2,1)S(1)}, u32[]{:S(2)}, u32[]{:S(2)}) collective-permute-start(bf16[2,192,256]{2,1,0:T(8,128)(2,1)} %bitcast.100), channel_id=1, source_target_pairs={{0,1},{1,0},{2,3},{3,2},{4,5},{5,4},{6,7},{7,6},{8,9},{9,8},{10,11... | collective-permute-start | bytes 589832 | tf_op jit(solution)/shard_map/ppermute | solution.py:8
  22.7 14.5 %copy-start.9 = (bf16[1,2,192,256]{3,2,1,0:T(8,128)(2,1)S(1)}, bf16[1,2,192,256]{3,2,1,0:T(8,128)(2,1)}, u32[]{:S(2)}) copy-start(bf16[1,2,192,256]{3,2,1,0:T(8,128)(2,1)} %param.10) | copy-start | bytes 589828
  25.9 489.0 %reduce-scatter.3.cloned.1.call-start = ((), (), s32[]{:S(2)}) async-start(), calls=%async_computation.3 | async-start | bytes 1114112 | tf_op jit(solution)/shard_map/reduce_scatter | solution.py:92
  27.2 7.9 %collective-permute-start.1 = (bf16[2,192,256]{2,1,0:T(8,128)(2,1)S(1)}, bf16[2,192,256]{2,1,0:T(8,128)(2,1)S(1)}, u32[]{:S(2)}, u32[]{:S(2)}) collective-permute-start(bf16[2,192,256]{2,1,0:T(8,128)(2,1)S(1)} %pad_maximum_fusion.7), channel_id=1, source_target_pairs={{0,2},{1,3},{2,0},{3,1},{4,6},{5,7},{6,4},{7,5},{8,10},{9,11},{10,... | collective-permute-start | bytes 589832 | tf_op jit(solution)/shard_map/ppermute | solution.py:8
  35.2 265.7 %collective-permute-start.2 = (bf16[2,192,512]{2,1,0:T(8,128)(2,1)S(1)}, bf16[2,192,512]{2,1,0:T(8,128)(2,1)S(1)}, u32[]{:S(2)}, u32[]{:S(2)}) collective-permute-start(bf16[2,192,512]{2,1,0:T(8,128)(2,1)S(1)} %pad_maximum_fusion.5), channel_id=1, source_target_pairs={{0,4},{1,5},{2,6},{3,7},{4,0},{5,1},{6,2},{7,3},{8,12},{9,13},{10,... | collective-permute-start | bytes 1179656 | tf_op jit(solution)/shard_map/ppermute | solution.py:8
  38.0 304.8 %collective-permute-start.5 = (bf16[2,192,512]{2,1,0:T(8,128)(2,1)}, bf16[2,192,512]{2,1,0:T(8,128)(2,1)}, u32[]{:S(2)}, u32[]{:S(2)}) collective-permute-start(bf16[2,192,512]{2,1,0:T(8,128)(2,1)} %pad_maximum_fusion.6), channel_id=1, source_target_pairs={{0,2},{1,3},{2,0},{3,1},{4,6},{5,7},{6,4},{7,5},{8,10},{9,11},{10,... | collective-permute-start | bytes 1179656 | tf_op jit(solution)/shard_map/ppermute | solution.py:8
  301.2 17.4 %collective-permute-start.3 = (bf16[2,192,1024]{2,1,0:T(8,128)(2,1)S(1)}, bf16[2,192,1024]{2,1,0:T(8,128)(2,1)}, u32[]{:S(2)}, u32[]{:S(2)}) collective-permute-start(bf16[2,192,1024]{2,1,0:T(8,128)(2,1)S(1)} %pad_maximum_fusion.3), channel_id=1, source_target_pairs={{0,8},{1,9},{2,10},{3,11},{4,12},{5,13},{6,14},{7,15},{8,0},{9,1},... | collective-permute-start | bytes 2359304 | tf_op jit(solution)/shard_map/ppermute | solution.py:8
  321.0 1.2 copy-start.6
  336.2 13.5 %copy-start.8 = (bf16[2,2,192,192]{2,3,1,0:T(8,128)(2,1)S(1)}, bf16[2,2,192,192]{2,3,1,0:T(8,128)(2,1)}, u32[]{:S(2)}) copy-start(bf16[2,2,192,192]{2,3,1,0:T(8,128)(2,1)} %all-reduce.2.cloned.1.call-done) | copy-start | bytes 884740
  336.2 10.6 %collective-permute-start.7 = (bf16[2,2,192,192]{3,2,1,0:T(8,128)(2,1)S(1)}, bf16[2,2,192,192]{3,2,1,0:T(8,128)(2,1)S(1)}, u32[]{:S(2)}, u32[]{:S(2)}) collective-permute-start(bf16[2,2,192,192]{3,2,1,0:T(8,128)(2,1)S(1)} %get-tuple-element.41), channel_id=1, source_target_pairs={{0,1},{1,0},{2,3},{3,2},{4,5},{5,4},{6,7},{7,6},{8,9},{9,8},{10,11... | collective-permute-start | bytes 884744 | tf_op jit(solution)/shard_map/ppermute | solution.py:8
  344.9 44.8 %collective-permute-start.6 = (bf16[2,192,1024]{2,1,0:T(8,128)(2,1)}, bf16[2,192,1024]{2,1,0:T(8,128)(2,1)}, u32[]{:S(2)}, u32[]{:S(2)}) collective-permute-start(bf16[2,192,1024]{2,1,0:T(8,128)(2,1)} %pad_maximum_fusion.4), channel_id=1, source_target_pairs={{0,4},{1,5},{2,6},{3,7},{4,0},{5,1},{6,2},{7,3},{8,12},{9,13},{10,... | collective-permute-start | bytes 2359304 | tf_op jit(solution)/shard_map/ppermute | solution.py:8
  346.8 26.1 %copy-start = (bf16[2,2,192,192]{3,2,1,0:T(8,128)(2,1)}, bf16[2,2,192,192]{3,2,1,0:T(8,128)(2,1)S(1)}, u32[]{:S(2)}) copy-start(bf16[2,2,192,192]{3,2,1,0:T(8,128)(2,1)S(1)} %collective-permute-done.7) | copy-start | bytes 884740
  347.8 25.0 %collective-permute-start.8 = (bf16[2,2,192,192]{3,2,1,0:T(8,128)(2,1)}, bf16[2,2,192,192]{3,2,1,0:T(8,128)(2,1)S(1)}, u32[]{:S(2)}, u32[]{:S(2)}) collective-permute-start(bf16[2,2,192,192]{3,2,1,0:T(8,128)(2,1)} %fusion.7), channel_id=1, source_target_pairs={{0,2},{1,3},{2,0},{3,1},{4,6},{5,7},{6,4},{7,5},{8,10},{9,11},{10,... | collective-permute-start | bytes 884744 | tf_op jit(solution)/shard_map/ppermute | solution.py:8
  372.8 18.4 %copy-start.4 = (bf16[2,2,192,192]{3,2,1,0:T(8,128)(2,1)}, bf16[2,2,192,192]{3,2,1,0:T(8,128)(2,1)S(1)}, u32[]{:S(2)}) copy-start(bf16[2,2,192,192]{3,2,1,0:T(8,128)(2,1)S(1)} %collective-permute-done.8) | copy-start | bytes 884740
  372.9 25.1 %collective-permute-start.9 = (bf16[2,2,192,192]{3,2,1,0:T(8,128)(2,1)S(1)}, bf16[2,2,192,192]{3,2,1,0:T(8,128)(2,1)S(1)}, u32[]{:S(2)}, u32[]{:S(2)}) collective-permute-start(bf16[2,2,192,192]{3,2,1,0:T(8,128)(2,1)S(1)} %fusion.17), channel_id=1, source_target_pairs={{0,4},{1,5},{2,6},{3,7},{4,0},{5,1},{6,2},{7,3},{8,12},{9,13},{10,... | collective-permute-start | bytes 884744 | tf_op jit(solution)/shard_map/ppermute | solution.py:8
  391.2 6.8 %copy-start.1 = (bf16[2,2,192,192]{3,2,1,0:T(8,128)(2,1)S(1)}, bf16[2,2,192,192]{3,2,1,0:T(8,128)(2,1)}, u32[]{:S(2)}) copy-start(bf16[2,2,192,192]{3,2,1,0:T(8,128)(2,1)} %copy-done) | copy-start | bytes 884740
  391.2 6.8 %copy-start.5 = (bf16[2,2,192,192]{3,2,1,0:T(8,128)(2,1)S(1)}, bf16[2,2,192,192]{3,2,1,0:T(8,128)(2,1)}, u32[]{:S(2)}) copy-start(bf16[2,2,192,192]{3,2,1,0:T(8,128)(2,1)} %copy-done.4) | copy-start | bytes 884740
  399.3 12.6 %copy-start.3 = (f32[2,2,192,192]{3,2,1,0:T(8,128)S(1)}, f32[2,2,192,192]{3,2,1,0:T(8,128)}, u32[]{:S(2)}) copy-start(f32[2,2,192,192]{3,2,1,0:T(8,128)} %get-tuple-element.5) | copy-start | bytes 1769476
  399.3 12.6 %collective-permute-start.10 = (bf16[2,2,192,192]{3,2,1,0:T(8,128)(2,1)}, bf16[2,2,192,192]{3,2,1,0:T(8,128)(2,1)}, u32[]{:S(2)}, u32[]{:S(2)}) collective-permute-start(bf16[2,2,192,192]{3,2,1,0:T(8,128)(2,1)} %get-tuple-element.4), channel_id=1, source_target_pairs={{0,8},{1,9},{2,10},{3,11},{4,12},{5,13},{6,14},{7,15},{8,0},{9,1},... | collective-permute-start | bytes 884744 | tf_op jit(solution)/shard_map/ppermute | solution.py:8
  403.8 9.3 %copy-start.7 = (bf16[192,2,192]{2,1,0:T(2,128)(2,1)S(1)}, bf16[192,2,192]{2,1,0:T(2,128)(2,1)}, u32[]{:S(2)}) copy-start(bf16[192,2,192]{2,1,0:T(2,128)(2,1)} %gather_fusion.4) | copy-start | bytes 442372
  403.8 10.3 %copy-start.10 = (bf16[1,2,192,256]{3,2,1,0:T(8,128)(2,1)S(1)}, bf16[1,2,192,256]{3,2,1,0:T(8,128)(2,1)}, u32[]{:S(2)}) copy-start(bf16[1,2,192,256]{3,2,1,0:T(8,128)(2,1)} %param.10) | copy-start | bytes 589828
  403.8 237.4 %reduce-scatter.5.cloned.1.call-start = ((), (), s32[]{:S(2)}) async-start(), calls=%async_computation.4 | async-start | bytes 2228224 | tf_op jit(solution)/shard_map/reduce_scatter | solution.py:132
  415.8 1.6 copy-start.2
Sparse Core Ops, SparseCore 0:
  26.1 273.8 all-reduce.1
  403.9 110.9 reduce-scatter.2
  519.6 121.5 reduce-scatter.4
where the time goes:
time: 649 us; the launch traced here: 648 us
  waiting for transfers between devices  539 us (83%)
  starting transfers between devices  33.5 us (5%)
  local copies, waits for them, and re-layouts  32.3 us (5%)
  other arithmetic  22.5 us (3%)
  between operations  14.5 us (2%)
    psum x1, waiting for transfers between devices, local(): blocks = lax.psum(pieces.astype(jnp.bfloat16), 'leaf').astype(jnp.float32)  260 us
    reduce_scatter x1, waiting for transfers between devices, local(): lax.psum_scatter(density_grand_term, 'pole', scatter_dimension=0, tiled=T...  126 us
    reduce_scatter x1, waiting for transfers between devices, local(): lax.psum_scatter(density_child_term, 'pole', scatter_dimension=0, tiled=T...  94 us
    ppermute x11, waiting for transfers between devices, partner_2(): lax.ppermute(x, axis, [(i, i ^ 1 << distance) for i in range(lax.axis_siz...  59.4 us
    ppermute x11, starting transfers between devices, partner_2(): lax.ppermute(x, axis, [(i, i ^ 1 << distance) for i in range(lax.axis_siz...  33.2 us
  transfers between devices with their start and end apart: 14, of which 9 were waited for; matrix products, arithmetic and copies ran while one was open for 9% of the time, Pallas kernels for 0%

commit v1 on v0

v1 whole, which is shorter than its diff:
```python
import jax
import jax.numpy as jnp
from jax import lax
from jax.experimental import pallas as pl
from jax.experimental.pallas import tpu as pltpu
from jax.sharding import PartitionSpec as P

MESH = pl.DeviceIdType.MESH
BF = jnp.bfloat16
F32 = jnp.float32


def mm(a, b):
    return jnp.dot(a, b, preferred_element_type=F32)


def mm_nt(a, b):
    return lax.dot_general(a, b, (((1,), (1,)), ((), ())), preferred_element_type=F32)


def hot(cond):
    return jnp.where(cond, 1.0, 0.0).astype(BF)


def column(row):
    return jnp.transpose(jnp.broadcast_to(row.astype(F32), (128, 128)))


def iota(shape, dim):
    return lax.broadcasted_iota(jnp.int32, shape, dim).astype(F32)


def twice(row):
    return jnp.concatenate([row, row], axis=1)


def row_of(ref, index, lanes):
    row = ref[0:1, lanes]
    for i in range(1, ref.shape[0]):
        row = jnp.where(index == i, ref[i : i + 1, lanes], row)
    return row


def right_side(off_re, off_im):
    re_col = jnp.concatenate([off_re[:128], -off_im[:128], off_re[128:], -off_im[128:]], axis=0)
    im_col = jnp.concatenate([off_im[:128], off_re[:128], off_im[128:], off_re[128:]], axis=0)
    return re_col, im_col


def transposed(ref, cols):
    parts = [
        ref[0, 0:128, cols],
        ref[1, 0:128, cols],
        jnp.concatenate([ref[0, 128:192, cols], ref[1, 128:192, cols]], axis=0),
    ]
    return jnp.concatenate([jnp.transpose(p.astype(F32)) for p in parts], axis=1).astype(BF)


def kernel(
    root,
    fc,
    fg,
    dc,
    dg,
    sc,
    sg,
    pw,
    out_c,
    out_g,
    root_v,
    fc_v,
    fg_v,
    dc_v,
    dg_v,
    ftc,
    ftg,
    oh,
    rl,
    t_send,
    t_recv,
    d_send,
    d_recv,
    part,
    rs_recv,
    full,
    acat,
    agcat,
    rhs_c,
    rhs_g,
    sx_c,
    sx_g,
    rx_c,
    rx_g,
    sz_c,
    sz_g,
    rz_c,
    rz_g,
    lsem,
    ty_s,
    ty_r,
    dy_s,
    dy_r,
    e3_s,
    e3_r,
    e4_s,
    e4_r,
    cz_s,
    cz_r,
    cy_s,
    cy_r,
    cc_s,
    cc_r,
    gz_s,
    gz_r,
    gc_s,
    gc_r,
    xc_s,
    xc_r,
    xg_s,
    xg_r,
    zc_s,
    zc_r,
    zg_s,
    zg_r,
):
    p = lax.axis_index("pole")
    leaf = lax.axis_index("leaf")
    x = p // 4
    zh = p % 4
    y = leaf // 8
    e = leaf % 8
    zl = e // 2
    k = e % 2
    c = y // 2
    yp = y % 2
    y_mate = y + 1 - 2 * yp
    base = y * 8

    def copy(src, dst, ssem, rsem, pole_to, leaf_to):
        return pltpu.make_async_remote_copy(
            src_ref=src,
            dst_ref=dst,
            send_sem=ssem,
            recv_sem=rsem,
            device_id=(pole_to, leaf_to),
            device_id_type=MESH,
        )

    def arrived(dst, rsem):
        copy(dst, dst, rsem, rsem, p, leaf).wait_recv()

    def sent(src, ssem):
        copy(src, src, ssem, ssem, p, leaf).wait_send()

    barrier = pltpu.get_barrier_semaphore()

    def greet(pole_to, leaf_to):
        pl.semaphore_signal(barrier, inc=1, device_id=(pole_to, leaf_to), device_id_type=MESH)

    for t in range(1, 4):
        greet(p, (y + t) % 4 * 8 + e)
        greet((x + t) % 4 * 4 + zh, leaf)
        greet(x * 4 + (zh + t) % 4, leaf)
    for t in range(1, 8):
        greet(p, base + (e + t) % 8)

    loads = [
        pltpu.make_async_copy(root.at[0, 0], root_v.at[0:64], lsem.at[0]),
        pltpu.make_async_copy(root.at[0, 1], root_v.at[64:128], lsem.at[1]),
        pltpu.make_async_copy(fc.at[0], fc_v, lsem.at[2]),
        pltpu.make_async_copy(fg.at[0], fg_v, lsem.at[3]),
        pltpu.make_async_copy(dc.at[0, 0], dc_v.at[:, 0:128], lsem.at[4]),
        pltpu.make_async_copy(dc.at[0, 1], dc_v.at[:, 128:256], lsem.at[5]),
        pltpu.make_async_copy(dg.at[0, 0], dg_v.at[:, 0:256], lsem.at[6]),
        pltpu.make_async_copy(dg.at[0, 1], dg_v.at[:, 256:512], lsem.at[7]),
    ]
    for load in loads:
        load.start()

    own_c = pl.multiple_of((yp * 8 + e) * 128, 128)
    own_g = pl.multiple_of(e * 256, 256)
    loads[2].wait()
    ftc[pl.ds(own_c, 128), :] = transposed(fc_v, slice(0, 128))
    loads[3].wait()
    ftg[pl.ds(own_g, 128), :] = transposed(fg_v, slice(0, 128))
    ftg[pl.ds(pl.multiple_of(own_g + 128, 128), 128), :] = transposed(fg_v, slice(128, 256))

    child_rows = [sc[0:1, 0:128], twice(sc[0:1, 128:192]), sc[1:2, 0:128], twice(sc[1:2, 128:192])]
    hot_rows = jnp.concatenate(child_rows, axis=1).astype(F32)

    def build_hot(i, carry):
        at = pl.multiple_of(i * 128, 128)
        ids = iota((128, 512), 0) + (i * 128).astype(F32)
        oh[pl.ds(at, 128), :] = hot(ids == hot_rows)
        return carry

    lax.fori_loop(0, 16, build_hot, 0)
    loads[0].wait()
    loads[1].wait()
    taken = mm(root_v[...], oh[...])
    low_lanes = iota((64, 128), 1) < 64
    for ch in range(2):
        at = ch * 256
        t_send[ch, 0:64, :] = taken[0:64, at : at + 128].astype(BF)
        t_send[ch, 64:128, :] = taken[64:128, at : at + 128].astype(BF)
        t_send[ch, 128:192, :] = jnp.where(
            low_lanes, taken[0:64, at + 128 : at + 256], taken[64:128, at + 128 : at + 256]
        ).astype(BF)

    pl.semaphore_wait(barrier, 16)

    for t in range(1, 4):
        y_to = (y + t) % 4
        copy(t_send.at[y_to // 2], t_recv.at[y], ty_s.at[t - 1], ty_r.at[y], p, y_to * 8 + e).start()
    t_recv[pl.ds(y, 1)] = t_send[pl.ds(c, 1)]

    def c_block(yy, j, kk):
        return ftc.at[pl.ds(pl.multiple_of((yy * 8 + j * 2 + kk) * 128, 128), 128)]

    def g_block(j, kk):
        return ftg.at[pl.ds(pl.multiple_of((j * 2 + kk) * 256, 256), 256)]

    def c_up(j):
        return copy(c_block(yp, j, k), c_block(yp, j, k), cz_s.at[j], cz_r.at[j], p, base + e + 2)

    def c_down(j):
        return copy(c_block(yp, j, k), c_block(yp, j, k), cz_s.at[4 + j], cz_r.at[j], p, base + e - 2)

    def c_side(j):
        return copy(c_block(yp, j, k), c_block(yp, j, k), cy_s.at[j], cy_r.at[j], p, y_mate * 8 + e)

    def c_core(yy, j):
        i = yy * 4 + j
        return copy(c_block(yy, j, k), c_block(yy, j, k), cc_s.at[i], cc_r.at[i], p, base + e + 1 - 2 * k)

    def g_up(j):
        return copy(g_block(j, k), g_block(j, k), gz_s.at[j], gz_r.at[j], p, base + e + 2)

    def g_down(j):
        return copy(g_block(j, k), g_block(j, k), gz_s.at[4 + j], gz_r.at[j], p, base + e - 2)

    def g_core(j):
        return copy(g_block(j, k), g_block(j, k), gc_s.at[j], gc_r.at[j], p, base + e + 1 - 2 * k)

    @pl.when(zl < 3)
    def _():
        c_up(zl).start()

    @pl.when(zl > 0)
    def _():
        c_down(zl).start()

    c_side(zl).start()
    c_core(yp, zl).start()

    @pl.when(zl < 3)
    def _():
        g_up(zl).start()

    @pl.when(zl > 0)
    def _():
        g_down(zl).start()

    g_core(zl).start()

    def c_relay(s):
        @pl.when(zl >= s)
        def _():
            j = zl - s
            arrived(c_block(yp, j, k), cz_r.at[j])

            @pl.when(zl < 3)
            def _():
                c_up(j).start()

            c_side(j).start()
            c_core(yp, j).start()

        @pl.when(zl + s <= 3)
        def _():
            j = zl + s
            arrived(c_block(yp, j, k), cz_r.at[j])

            @pl.when(zl > 0)
            def _():
                c_down(j).start()

            c_side(j).start()
            c_core(yp, j).start()

    def g_relay(s):
        @pl.when(zl >= s)
        def _():
            j = zl - s
            arrived(g_block(j, k), gz_r.at[j])

            @pl.when(zl < 3)
            def _():
                g_up(j).start()

            g_core(j).start()

        @pl.when(zl + s <= 3)
        def _():
            j = zl + s
            arrived(g_block(j, k), gz_r.at[j])

            @pl.when(zl > 0)
            def _():
                g_down(j).start()

            g_core(j).start()

    col0 = column(row_of(sg, y, slice(0, 128)))
    col1 = column(twice(row_of(sg, y, slice(128, 192))))
    col_mate = column(row_of(sg, y_mate, slice(0, 128)))
    lane = iota((128, 128), 1)

    def build_low(i, carry):
        at = pl.multiple_of(i * 128, 128)
        ids = lane + (i * 128).astype(F32)
        rl[0:128, pl.ds(at, 128)] = hot(col0 == ids)
        rl[128:256, pl.ds(at, 128)] = hot(col_mate == ids)
        return carry

    lax.fori_loop(0, 16, build_low, 0)
    loads[4].wait()
    loads[5].wait()
    picked = mm(rl[...], dc_v[...]).astype(BF)
    own_ids = iota((128, 128), 0) + own_c.astype(F32)
    pick_own = hot(own_ids == row_of(sg, y, slice(0, 128)).astype(F32))
    pick_mate = hot(own_ids == row_of(sg, y_mate, slice(0, 128)).astype(F32))
    d_send[0:96, :] = mm(picked[128:224, 0:128], pick_mate).astype(BF)
    d_send[96:192, :] = mm(picked[128:224, 128:256], pick_mate).astype(BF)
    copy(d_send, d_recv, dy_s.at[0], dy_r.at[0], p, y_mate * 8 + e).start()
    d_re = mm(picked[0:96, 0:128], pick_own)
    d_im = mm(picked[0:96, 128:256], pick_own)

    a_row0 = column(row_of(sc, c, slice(0, 128)))
    a_row1 = column(twice(row_of(sc, c, slice(128, 192))))
    lane_at = jnp.where(lane < 64, lane, lane + 448.0) + (e * 64).astype(F32)
    fold = jnp.concatenate(
        [
            jnp.concatenate([hot(a_row0 == lane_at), hot(a_row0 == lane_at + 1024.0)], axis=1),
            jnp.concatenate([hot(a_row1 == lane_at), hot(a_row1 == lane_at + 1024.0)], axis=1)[0:64],
        ],
        axis=0,
    )
    for t in range(1, 4):
        y_from = (y + t) % 4
        arrived(t_recv.at[y_from], ty_r.at[y_from])
    for b in range(3):
        raw = jnp.concatenate([t_recv[i, b * 64 : b * 64 + 64, :] for i in range(4)], axis=0)
        part[b * 192 : b * 192 + 192, :] = mm(fold, raw).astype(BF)
    arrived(d_recv, dy_r.at[0])
    part[576:672, :] = (d_re + d_recv[0:96, :].astype(F32)).astype(BF)
    part[672:768, :] = (d_im + d_recv[96:192, :].astype(F32)).astype(BF)

    def piece(ref, i):
        return ref.at[pl.ds(pl.multiple_of(i * 96, 96), 96)]

    for t in range(1, 8):
        to = (e + t) % 8
        copy(piece(part, to), rs_recv.at[e], e3_s.at[t - 1], e3_r.at[e], p, base + to).start()
    c_relay(1)
    total = part[pl.ds(pl.multiple_of(e * 96, 96), 96), :].astype(F32)
    for t in range(1, 8):
        at = (e + t) % 8
        arrived(rs_recv.at[at], e3_r.at[at])
        total = total + rs_recv[at].astype(F32)
    full[pl.ds(pl.multiple_of(e * 96, 96), 96), :] = total.astype(BF)

    for t in range(1, 8):
        to = (e + t) % 8
        copy(piece(full, e), piece(full, e), e4_s.at[t - 1], e4_r.at[e], p, base + to).start()
    c_relay(2)
    g_relay(1)
    for t in range(1, 8):
        at = (e + t) % 8
        arrived(piece(full, at), e4_r.at[at])
    for b in range(3):
        acat[:, b * 128 : b * 128 + 128] = full[b * 192 : b * 192 + 192, :]

    g_re, g_im = right_side(fc_v[0], fc_v[1])
    a_now = acat[...]
    off_re = (-mm(a_now, g_re)).astype(BF)
    off_im = (-mm(a_now, g_im)).astype(BF)
    r_re, r_im = right_side(off_re, off_im)
    rhs_c[:, 0:128] = r_re
    rhs_c[:, 128:256] = r_im

    c_relay(3)
    for i in range(4):
        arrived(c_block(1 - yp, i, k), cy_r.at[i])
        c_core(1 - yp, i).start()
    for i in range(8):
        arrived(c_block(i // 4, i % 4, 1 - k), cc_r.at[i])

    ft_r = mm(rl[0:128, :], ftc[...])
    lane384 = lax.broadcasted_iota(jnp.int32, (128, 384), 1)
    is_im = ((lane384 >= 128) & (lane384 < 256)) | (lane384 >= 320)
    f_re = jnp.where(is_im, -ft_r, ft_r).astype(BF)
    f_im = jnp.concatenate(
        [ft_r[:, 128:256], ft_r[:, 0:128], pltpu.roll(ft_r[:, 256:384], 64, 1)], axis=1
    ).astype(BF)
    a_low = acat[0:128, :]
    a_high = jnp.concatenate([acat[128:192, :], acat[128:192, :]], axis=0)
    off_t = jnp.concatenate(
        [
            -mm_nt(f_re, a_low),
            -mm_nt(f_im, a_low),
            -jnp.where(lane < 64, mm_nt(f_re, a_high), mm_nt(f_im, a_high)),
        ],
        axis=1,
    ).astype(BF)
    none = jnp.zeros((128, 128), BF)
    up0 = col0 - 2048.0
    up1 = col1 - 2048.0
    lane_hi = jnp.where(lane < 64, lane, lane - 64.0) + 128.0
    near0 = hot(up0 == lane)
    near1 = hot(up1 == lane)
    far0 = up0 == lane_hi
    far1 = up1 == lane_hi
    sub = iota((128, 128), 0)
    q0 = jnp.concatenate([near0, none, hot(far0 & (lane < 64))], axis=1)
    q1 = jnp.concatenate([none, near0, hot(far0 & (lane >= 64))], axis=1)
    q2 = jnp.concatenate(
        [
            jnp.where(sub < 64, near1.astype(F32), 0.0).astype(BF),
            jnp.where(sub >= 64, near1.astype(F32), 0.0).astype(BF),
            hot(far1 & ((lane < 64) == (sub < 64))),
        ],
        axis=1,
    )
    up_near = jnp.concatenate([near0, near1[0:64]], axis=0)
    up_far = jnp.concatenate([hot(far0), hot(far1)[0:64]], axis=0)[:, 0:64]
    a_rows = mm(up_near, acat[0:128, :]) + mm(up_far, acat[128:192, :])
    rows_all = a_rows + jnp.concatenate([off_t.astype(F32), jnp.zeros((64, 384), F32)], axis=0)
    q_all = jnp.concatenate([q0, q1, q2], axis=0)
    ag = mm_nt(rows_all.astype(BF), q_all)
    up_re = jnp.concatenate([q0, q2[0:64]], axis=0)
    up_im = jnp.concatenate([q1, q2[64:128]], axis=0)
    rest = jnp.zeros((32, 128), F32)
    tail = jnp.zeros((64, 128), F32)
    in_re = jnp.concatenate([full[576:672, :].astype(F32), rest], axis=0) - mm_nt(f_re, off_t)
    in_im = jnp.concatenate([full[672:768, :].astype(F32), rest], axis=0) - mm_nt(f_im, off_t)
    agcat[:, 0:128] = (
        ag[:, 0:128] + mm_nt(up_re, off_t) + jnp.concatenate([in_re, tail], axis=0)
    ).astype(BF)
    agcat[:, 128:256] = (
        ag[:, 128:256] + mm_nt(up_im, off_t) + jnp.concatenate([in_im, tail], axis=0)
    ).astype(BF)
    agcat[:, 256:384] = ag[:, 256:384].astype(BF)

    g_relay(2)

    gg_re, gg_im = right_side(fg_v[0], fg_v[1])
    ag_now = agcat[...]
    goff_re = (-mm(ag_now, gg_re)).astype(BF)
    goff_im = (-mm(ag_now, gg_im)).astype(BF)
    r_re, r_im = right_side(goff_re, goff_im)
    rhs_g[:, 0:256] = r_re
    rhs_g[:, 256:512] = r_im

    w_im = pw[0, 0]
    w_re = pw[0, 1]

    def density(acc, diag, n):
        re = (diag[:, 0:n].astype(F32) - acc[:, 0:n]).astype(BF).astype(F32)
        im = (diag[:, n : 2 * n].astype(F32) - acc[:, n : 2 * n]).astype(BF).astype(F32)
        return (w_im * im + w_re * re).astype(BF)

    for t in range(1, 5):
        x_to = (x + t) % 4

        def c_rows(i, carry, x_to=x_to):
            at = pl.multiple_of(i * 256, 256)
            rows = pl.ds(pl.multiple_of(x_to * 512 + i * 256, 256), 256)
            sx_c[x_to, pl.ds(at, 256), :] = density(mm(ftc[rows, :], rhs_c[...]), dc_v[rows, :], 128)
            return carry

        lax.fori_loop(0, 2, c_rows, 0)
        if t < 4:
            copy(sx_c.at[x_to], rx_c.at[x], xc_s.at[t - 1], xc_r.at[x], x_to * 4 + zh, leaf).start()

    g_relay(3)
    for i in range(4):
        arrived(g_block(i, 1 - k), gc_r.at[i])
    loads[6].wait()
    loads[7].wait()

    for t in range(1, 5):
        x_to = (x + t) % 4

        def g_rows(i, carry, x_to=x_to):
            at = pl.multiple_of(i * 256, 256)
            rows = pl.ds(pl.multiple_of(x_to * 512 + i * 256, 256), 256)
            sx_g[x_to, pl.ds(at, 256), :] = density(mm(ftg[rows, :], rhs_g[...]), dg_v[rows, :], 256)
            return carry

        lax.fori_loop(0, 2, g_rows, 0)
        if t < 4:
            copy(sx_g.at[x_to], rx_g.at[x], xg_s.at[t - 1], xg_r.at[x], x_to * 4 + zh, leaf).start()

    def along_z(sx, rx, sz, rz, xr, zs, zr):
        for t in range(1, 4):
            x_from = (x + t) % 4
            arrived(rx.at[x_from], xr.at[x_from])
        for t in range(1, 5):
            to = (zh + t) % 4
            rows = pl.ds(pl.multiple_of(to * 128, 128), 128)
            total = sx[x, rows, :].astype(F32)
            for u in range(1, 4):
                total = total + rx[(x + u) % 4, rows, :].astype(F32)
            if t < 4:
                sz[to] = total.astype(BF)
                copy(sz.at[to], rz.at[zh], zs.at[t - 1], zr.at[zh], x * 4 + to, leaf).start()
        return total

    own_cs = along_z(sx_c, rx_c, sz_c, rz_c, xc_r, zc_s, zc_r)
    own_gs = along_z(sx_g, rx_g, sz_g, rz_g, xg_r, zg_s, zg_r)
    for t in range(1, 4):
        z_from = (zh + t) % 4
        arrived(rz_c.at[z_from], zc_r.at[z_from])
        own_cs = own_cs + rz_c[z_from].astype(F32)
    out_c[...] = own_cs
    for t in range(1, 4):
        z_from = (zh + t) % 4
        arrived(rz_g.at[z_from], zg_r.at[z_from])
        own_gs = own_gs + rz_g[z_from].astype(F32)
    out_g[...] = own_gs

    for t in range(3):
        sent(t_send.at[0], ty_s.at[t])
        sent(sx_c.at[0], xc_s.at[t])
        sent(sx_g.at[0], xg_s.at[t])
        sent(sz_c.at[0], zc_s.at[t])
        sent(sz_g.at[0], zg_s.at[t])
    sent(d_send, dy_s.at[0])
    for t in range(7):
        sent(piece(part, 0), e3_s.at[t])
        sent(piece(full, 0), e4_s.at[t])
    for j in range(4):

        @pl.when((zl < 3) & (j <= zl))
        def _(j=j):
            sent(c_block(0, 0, 0), cz_s.at[j])
            sent(g_block(0, 0), gz_s.at[j])

        @pl.when((zl > 0) & (j >= zl))
        def _(j=j):
            sent(c_block(0, 0, 0), cz_s.at[4 + j])
            sent(g_block(0, 0), gz_s.at[4 + j])

        sent(c_block(0, 0, 0), cy_s.at[j])
        sent(c_block(0, 0, 0), cc_s.at[j])
        sent(c_block(0, 0, 0), cc_s.at[4 + j])
        sent(g_block(0, 0), gc_s.at[j])


def local(*args):
    vm = pltpu.VMEM
    dma = pltpu.SemaphoreType.DMA
    scratch = [
        vm((128, 2048), BF),
        vm((2, 192, 128), BF),
        vm((2, 192, 256), BF),
        vm((2048, 256), BF),
        vm((2048, 512), BF),
        vm((2048, 384), BF),
        vm((2048, 384), BF),
        vm((2048, 512), BF),
        vm((256, 2048), BF),
        vm((2, 192, 128), BF),
        vm((4, 192, 128), BF),
        vm((192, 128), BF),
        vm((192, 128), BF),
        vm((768, 128), BF),
        vm((8, 96, 128), BF),
        vm((768, 128), BF),
        vm((192, 384), BF),
        vm((192, 384), BF),
        vm((384, 256), BF),
        vm((384, 512), BF),
        vm((4, 512, 128), BF),
        vm((4, 512, 256), BF),
        vm((4, 512, 128), BF),
        vm((4, 512, 256), BF),
        vm((4, 128, 128), BF),
        vm((4, 128, 256), BF),
        vm((4, 128, 128), BF),
        vm((4, 128, 256), BF),
        dma((8,)),
        dma((3,)),
        dma((4,)),
        dma((1,)),
        dma((1,)),
        dma((7,)),
        dma((8,)),
        dma((7,)),
        dma((8,)),
        dma((8,)),
        dma((4,)),
        dma((4,)),
        dma((4,)),
        dma((8,)),
        dma((8,)),
        dma((8,)),
        dma((4,)),
        dma((4,)),
        dma((4,)),
        dma((3,)),
        dma((4,)),
        dma((3,)),
        dma((4,)),
        dma((3,)),
        dma((4,)),
        dma((3,)),
        dma((4,)),
    ]
    any_spec = pl.BlockSpec(memory_space=pl.ANY)
    vm_spec = pl.BlockSpec(memory_space=pltpu.VMEM)
    return pl.pallas_call(
        kernel,
        out_shape=[
            jax.ShapeDtypeStruct((128, 128), F32),
            jax.ShapeDtypeStruct((128, 256), F32),
        ],
        in_specs=[any_spec] * 5 + [vm_spec] * 2 + [pl.BlockSpec(memory_space=pltpu.SMEM)],
        out_specs=[vm_spec, vm_spec],
        scratch_shapes=scratch,
        compiler_params=pltpu.CompilerParams(
            collective_id=0, has_side_effects=True, vmem_limit_bytes=40 * 1024 * 1024
        ),
        cost_estimate=pl.CostEstimate(flops=3_000_000_000, bytes_accessed=5_000_000, transcendentals=0),
    )(*args)


def solution(mesh):
    placed = (
        P("pole", None, "leaf", None),
        P("pole", None, None, "leaf"),
        P("pole", None, None, "leaf"),
        P("pole", None, None, "leaf"),
        P("pole", None, None, "leaf"),
        P(),
        P(),
        P("pole", None),
    )
    return jax.shard_map(
        local,
        mesh=mesh,
        in_specs=placed,
        out_specs=(P("pole", "leaf"), P("pole", "leaf")),
        check_vma=False,
    )
```

time: 649 us -> 87.2 us (0.13)
  waiting for transfers between devices: 539 us -> 0 us
  Pallas kernels: 0 us -> 77.2 us
  starting transfers between devices: 33.5 us -> 0 us
  local copies, waits for them, and re-layouts: 32.3 us -> 8.98 us
  other arithmetic: 22.5 us -> 0 us
  between operations: 14.5 us -> 0.66 us
    psum x1 -> x0, waiting for transfers between devices: 260 us -> none  [local(): blocks = lax.psum(pieces.astype(jnp.bfloat16), 'leaf').astype(jnp.float32)]
    reduce_scatter x2 -> x0, waiting for transfers between devices: 220 us -> none  [the longest x1 126 us: local(): lax.psum_scatter(density_grand_term, 'pole', scatter_dimension=0, tiled=T...]
    pallas_call x0 -> x1, Pallas kernels: none -> 77.2 us  [local(): pl.pallas_call(kernel, out_shape=[jax.ShapeDtypeStruct((128, 128), F32),...]
    ppermute x11 -> x0, waiting for transfers between devices: 59.4 us -> none  [partner_2(): lax.ppermute(x, axis, [(i, i ^ 1 << distance) for i in range(lax.axis_siz...]
    ppermute x11 -> x0, starting transfers between devices: 33.2 us -> none  [partner_2(): lax.ppermute(x, axis, [(i, i ^ 1 << distance) for i in range(lax.axis_siz...]
    gather x6 -> x0, local copies, waits for them, and re-layouts: 12 us -> none  [the longest x1 2.71 us: local(): jnp.take(ancestor, local_index, axis=1)]
    concatenate x1 -> x0, local copies, waits for them, and re-layouts: 9.87 us -> none  [local(): ext_cols = jnp.concatenate([child_inverse, child_off], axis=1)]
    select_n x10 -> x0, other arithmetic: 7 us -> none  [the longest x7 4.39 us: ordered_join(): first_part = jnp.where(lower_half, own_piece, partner)]
  transfers between devices with their start and end apart: 14 -> 0, of which waited for: 9 -> 0; matrix products, arithmetic and copies ran while one was open for 9% -> 0% of each run, Pallas kernels for 0% -> 0%
where the time goes in v1:
time: 87.2 us; the launch traced here: 86.8 us
  Pallas kernels  77.2 us (89%)
  local copies, waits for them, and re-layouts  8.98 us (10%)
    pallas_call x1, Pallas kernels, local(): pl.pallas_call(kernel, out_shape=[jax.ShapeDtypeStruct((128, 128), F32),...  77.2 us
    unnamed x18, local copies, waits for them, and re-layouts  8.98 us

profile of v1, /device:TPU:1, one launch (start us, length us, event | category | flops | bytes accessed | tf_op | source)
XLA Modules:
  0.0 86.8 jit_solution(15806570345015159432)
XLA Ops:
  0.6 0.0 copy-start
  0.6 1.6 %copy-done = bf16[1,2,2048,256]{3,2,1,0:T(8,128)(2,1)S(1)} copy-done((bf16[1,2,2048,256]{3,2,1,0:T(8,128)(2,1)S(1)}, bf16[1,2,2048,256]{3,2,1,0:T(8,128)(2,1)}, u32[]{:S(2)}) %copy-start) | copy-done | bytes 2097176
  2.2 0.0 copy-start.1
  2.2 1.2 %copy-done.1 = bf16[1,2,2048,128]{3,2,1,0:T(8,128)(2,1)S(1)} copy-done((bf16[1,2,2048,128]{3,2,1,0:T(8,128)(2,1)S(1)}, bf16[1,2,2048,128]{3,2,1,0:T(8,128)(2,1)}, u32[]{:S(2)}) %copy-start.1) | copy-done | bytes 1048600
  3.5 0.0 copy-start.2
  3.5 1.0 %copy-done.2 = bf16[1,2,64,2048]{3,2,1,0:T(8,128)(2,1)S(1)} copy-done((bf16[1,2,64,2048]{3,2,1,0:T(8,128)(2,1)S(1)}, bf16[1,2,64,2048]{3,2,1,0:T(8,128)(2,1)}, u32[]{:S(2)}) %copy-start.2) | copy-done | bytes 524312
  4.5 0.0 copy-start.3
  4.5 0.9 %copy-done.3 = bf16[1,2,192,256]{3,2,1,0:T(8,128)(2,1)S(1)} copy-done((bf16[1,2,192,256]{3,2,1,0:T(8,128)(2,1)S(1)}, bf16[1,2,192,256]{3,2,1,0:T(8,128)(2,1)}, u32[]{:S(2)}) %copy-start.3) | copy-done | bytes 196632
  5.4 0.0 copy-start.4
  5.4 0.9 %copy-done.4 = bf16[1,2,192,128]{3,2,1,0:T(8,128)(2,1)S(1)} copy-done((bf16[1,2,192,128]{3,2,1,0:T(8,128)(2,1)S(1)}, bf16[1,2,192,128]{3,2,1,0:T(8,128)(2,1)}, u32[]{:S(2)}) %copy-start.4) | copy-done | bytes 98328
  6.3 0.0 copy-start.5
  6.3 0.7 copy-done.5
  7.0 0.0 copy-start.6
  7.0 0.7 copy-done.6
  7.7 0.0 copy-start.7
  7.7 0.7 copy-done.7
  8.3 77.2 %shard_map.95 = (f32[128,128]{1,0:T(8,128)S(1)}, f32[128,256]{1,0:T(8,128)S(1)}) custom-call(bf16[1,2,64,2048]{3,2,1,0:T(8,128)(2,1)S(1)} %copy-done.2, bf16[1,2,192,128]{3,2,1,0:T(8,128)(2,1)S(1)} %copy-done.4, bf16[1,2,192,256]{3,2,1,0:T(8,128)(2,1)S(1)} %copy-done.3, bf16[1,2,2048,128]{3,2,1,0:T(8,128)(2,1)S(1)} %copy-done.1, ...), custom_call_target="tpu_custom_call" | custom-call | flops 3000000000 | bytes 5000000 | tf_op jit(solution)/shard_map/pallas_call | solution.py:623
  85.5 0.6 copy.12
  86.1 0.7 copy.13
Async XLA Ops:
  0.6 1.6 %copy-start = (bf16[1,2,2048,256]{3,2,1,0:T(8,128)(2,1)S(1)}, bf16[1,2,2048,256]{3,2,1,0:T(8,128)(2,1)}, u32[]{:S(2)}) copy-start(bf16[1,2,2048,256]{3,2,1,0:T(8,128)(2,1)} %dg.1) | copy-start | bytes 6291460
  2.2 1.2 %copy-start.1 = (bf16[1,2,2048,128]{3,2,1,0:T(8,128)(2,1)S(1)}, bf16[1,2,2048,128]{3,2,1,0:T(8,128)(2,1)}, u32[]{:S(2)}) copy-start(bf16[1,2,2048,128]{3,2,1,0:T(8,128)(2,1)} %dc.1) | copy-start | bytes 3145732
  3.5 1.0 %copy-start.2 = (bf16[1,2,64,2048]{3,2,1,0:T(8,128)(2,1)S(1)}, bf16[1,2,64,2048]{3,2,1,0:T(8,128)(2,1)}, u32[]{:S(2)}) copy-start(bf16[1,2,64,2048]{3,2,1,0:T(8,128)(2,1)} %root.1) | copy-start | bytes 1572868
  4.5 0.9 %copy-start.3 = (bf16[1,2,192,256]{3,2,1,0:T(8,128)(2,1)S(1)}, bf16[1,2,192,256]{3,2,1,0:T(8,128)(2,1)}, u32[]{:S(2)}) copy-start(bf16[1,2,192,256]{3,2,1,0:T(8,128)(2,1)} %fg.1) | copy-start | bytes 589828
  5.4 0.9 %copy-start.4 = (bf16[1,2,192,128]{3,2,1,0:T(8,128)(2,1)S(1)}, bf16[1,2,192,128]{3,2,1,0:T(8,128)(2,1)}, u32[]{:S(2)}) copy-start(bf16[1,2,192,128]{3,2,1,0:T(8,128)(2,1)} %fc.1) | copy-start | bytes 294916
  6.3 0.7 copy-start.5
  7.0 0.7 copy-start.6
  7.7 0.7 copy-start.7

commit v2 on v1

--- a/solution.py
+++ b/solution.py
@@ -62,16 +62,18 @@
     fg,
     dc,
     dg,
+    sc_hbm,
+    sg_hbm,
+    pw_hbm,
+    out_c,
+    out_g,
     sc,
     sg,
     pw,
-    out_c,
-    out_g,
     root_v,
     fc_v,
     fg_v,
-    dc_v,
-    dg_v,
+    diag_v,
     ftc,
     ftg,
     oh,
@@ -85,16 +87,15 @@
     full,
     acat,
     agcat,
-    rhs_c,
-    rhs_g,
-    sx_c,
-    sx_g,
-    rx_c,
-    rx_g,
-    sz_c,
-    sz_g,
-    rz_c,
-    rz_g,
+    rhs,
+    s_opp,
+    r_opp,
+    s_nb,
+    r_nb,
+    own,
+    sz,
+    rz,
+    keep,
     lsem,
     ty_s,
     ty_r,
@@ -114,14 +115,12 @@
     gz_r,
     gc_s,
     gc_r,
-    xc_s,
-    xc_r,
-    xg_s,
-    xg_r,
-    zc_s,
-    zc_r,
-    zg_s,
-    zg_r,
+    op_s,
+    op_r,
+    nb_s,
+    nb_r,
+    z_s,
+    z_r,
 ):
     p = lax.axis_index("pole")
     leaf = lax.axis_index("leaf")
@@ -169,13 +168,18 @@
         pltpu.make_async_copy(root.at[0, 1], root_v.at[64:128], lsem.at[1]),
         pltpu.make_async_copy(fc.at[0], fc_v, lsem.at[2]),
         pltpu.make_async_copy(fg.at[0], fg_v, lsem.at[3]),
-        pltpu.make_async_copy(dc.at[0, 0], dc_v.at[:, 0:128], lsem.at[4]),
-        pltpu.make_async_copy(dc.at[0, 1], dc_v.at[:, 128:256], lsem.at[5]),
-        pltpu.make_async_copy(dg.at[0, 0], dg_v.at[:, 0:256], lsem.at[6]),
-        pltpu.make_async_copy(dg.at[0, 1], dg_v.at[:, 256:512], lsem.at[7]),
+        pltpu.make_async_copy(dc.at[0, 0], diag_v.at[0, :, 0:128], lsem.at[4]),
+        pltpu.make_async_copy(dc.at[0, 1], diag_v.at[0, :, 128:256], lsem.at[5]),
+        pltpu.make_async_copy(dg.at[0, 0, :, 0:128], diag_v.at[1, :, 0:128], lsem.at[6]),
+        pltpu.make_async_copy(dg.at[0, 1, :, 0:128], diag_v.at[1, :, 128:256], lsem.at[7]),
+        pltpu.make_async_copy(sc_hbm, sc, lsem.at[8]),
+        pltpu.make_async_copy(sg_hbm, sg, lsem.at[9]),
+        pltpu.make_async_copy(pw_hbm, pw, lsem.at[10]),
+        pltpu.make_async_copy(dg.at[0, 0, :, 128:256], diag_v.at[2, :, 0:128], lsem.at[11]),
+        pltpu.make_async_copy(dg.at[0, 1, :, 128:256], diag_v.at[2, :, 128:256], lsem.at[12]),
     ]
-    for load in loads:
-        load.start()
+    for i in (8, 9, 2, 3, 0, 1, 4, 5, 10, 6, 7, 11, 12):
+        loads[i].start()
 
     own_c = pl.multiple_of((yp * 8 + e) * 128, 128)
     own_g = pl.multiple_of(e * 256, 256)
@@ -185,6 +189,9 @@
     ftg[pl.ds(own_g, 128), :] = transposed(fg_v, slice(0, 128))
     ftg[pl.ds(pl.multiple_of(own_g + 128, 128), 128), :] = transposed(fg_v, slice(128, 256))
 
+    loads[8].wait()
+    loads[9].wait()
+    loads[10].wait()
     child_rows = [sc[0:1, 0:128], twice(sc[0:1, 128:192]), sc[1:2, 0:128], twice(sc[1:2, 128:192])]
     hot_rows = jnp.concatenate(child_rows, axis=1).astype(F32)
 
@@ -242,26 +249,28 @@
     def g_core(j):
         return copy(g_block(j, k), g_block(j, k), gc_s.at[j], gc_r.at[j], p, base + e + 1 - 2 * k)
 
-    @pl.when(zl < 3)
-    def _():
-        c_up(zl).start()
-
-    @pl.when(zl > 0)
-    def _():
-        c_down(zl).start()
-
-    c_side(zl).start()
-    c_core(yp, zl).start()
-
-    @pl.when(zl < 3)
-    def _():
-        g_up(zl).start()
-
-    @pl.when(zl > 0)
-    def _():
-        g_down(zl).start()
-
-    g_core(zl).start()
+    def c_first():
+        @pl.when(zl < 3)
+        def _():
+            c_up(zl).start()
+
+        @pl.when(zl > 0)
+        def _():
+            c_down(zl).start()
+
+        c_side(zl).start()
+        c_core(yp, zl).start()
+
+    def g_first():
+        @pl.when(zl < 3)
+        def _():
+            g_up(zl).start()
+
+        @pl.when(zl > 0)
+        def _():
+            g_down(zl).start()
+
+        g_core(zl).start()
 
     def c_relay(s):
         @pl.when(zl >= s)
@@ -310,6 +319,20 @@
                 g_down(j).start()
 
             g_core(j).start()
+
+    def c_finish():
+        for i in range(4):
+            arrived(c_block(1 - yp, i, k), cy_r.at[i])
+            c_core(1 - yp, i).start()
+        for i in range(8):
+            arrived(c_block(i // 4, i % 4, 1 - k), cc_r.at[i])
+
+    def g_finish():
+        for i in range(4):
+            arrived(g_block(i, 1 - k), gc_r.at[i])
+
+    c_first()
+    g_first()
 
     col0 = column(row_of(sg, y, slice(0, 128)))
     col1 = column(twice(row_of(sg, y, slice(128, 192))))
@@ -326,7 +349,7 @@
     lax.fori_loop(0, 16, build_low, 0)
     loads[4].wait()
     loads[5].wait()
-    picked = mm(rl[...], dc_v[...]).astype(BF)
+    picked = mm(rl[...], diag_v[0]).astype(BF)
     own_ids = iota((128, 128), 0) + own_c.astype(F32)
     pick_own = hot(own_ids == row_of(sg, y, slice(0, 128)).astype(F32))
     pick_mate = hot(own_ids == row_of(sg, y_mate, slice(0, 128)).astype(F32))
@@ -386,15 +409,11 @@
     off_re = (-mm(a_now, g_re)).astype(BF)
     off_im = (-mm(a_now, g_im)).astype(BF)
     r_re, r_im = right_side(off_re, off_im)
-    rhs_c[:, 0:128] = r_re
-    rhs_c[:, 128:256] = r_im
+    rhs[0, :, 0:128] = r_re
+    rhs[0, :, 128:256] = r_im
 
     c_relay(3)
-    for i in range(4):
-        arrived(c_block(1 - yp, i, k), cy_r.at[i])
-        c_core(1 - yp, i).start()
-    for i in range(8):
-        arrived(c_block(i // 4, i % 4, 1 - k), cc_r.at[i])
+    c_finish()
 
     ft_r = mm(rl[0:128, :], ftc[...])
     lane384 = lax.broadcasted_iota(jnp.int32, (128, 384), 1)
@@ -459,83 +478,108 @@
     goff_re = (-mm(ag_now, gg_re)).astype(BF)
     goff_im = (-mm(ag_now, gg_im)).astype(BF)
     r_re, r_im = right_side(goff_re, goff_im)
-    rhs_g[:, 0:256] = r_re
-    rhs_g[:, 256:512] = r_im
+    for h in range(2):
+        rhs[1 + h, :, 0:128] = r_re[:, h * 128 : h * 128 + 128]
+        rhs[1 + h, :, 128:256] = r_im[:, h * 128 : h * 128 + 128]
 
     w_im = pw[0, 0]
     w_re = pw[0, 1]
 
-    def density(acc, diag, n):
-        re = (diag[:, 0:n].astype(F32) - acc[:, 0:n]).astype(BF).astype(F32)
-        im = (diag[:, n : 2 * n].astype(F32) - acc[:, n : 2 * n]).astype(BF).astype(F32)
-        return (w_im * im + w_re * re).astype(BF)
-
-    for t in range(1, 5):
-        x_to = (x + t) % 4
-
-        def c_rows(i, carry, x_to=x_to):
-            at = pl.multiple_of(i * 256, 256)
-            rows = pl.ds(pl.multiple_of(x_to * 512 + i * 256, 256), 256)
-            sx_c[x_to, pl.ds(at, 256), :] = density(mm(ftc[rows, :], rhs_c[...]), dc_v[rows, :], 128)
-            return carry
-
-        lax.fori_loop(0, 2, c_rows, 0)
-        if t < 4:
-            copy(sx_c.at[x_to], rx_c.at[x], xc_s.at[t - 1], xc_r.at[x], x_to * 4 + zh, leaf).start()
+    def density(i, quarter, half):
+        rows = pl.ds(pl.multiple_of(quarter * 512 + half * 256, 256), 256)
+        ft = ftc[rows, :] if i == 0 else ftg[rows, :]
+        rest_of = diag_v[i, rows, :].astype(F32) - mm(ft, rhs[i])
+        rest_of = rest_of.astype(BF).astype(F32)
+        return w_im * rest_of[:, 128:256] + w_re * rest_of[:, 0:128]
+
+    x_next = (x + 1) % 4
+    x_prev = (x + 3) % 4
+    x_far = (x + 2) % 4
+    p_next = x_next * 4 + zh
+    p_prev = x_prev * 4 + zh
+
+    def half_of(ref, h):
+        return ref.at[pl.ds(h * 256, 256)]
+
+    def opposite(i):
+        for h, to in ((0, p_next), (1, p_prev)):
+            s_opp[i, h] = density(i, x_far, h).astype(BF)
+            copy(s_opp.at[i, h], r_opp.at[i, h], op_s.at[i, h], op_r.at[i, h], to, leaf).start()
+
+    def neighbours(i):
+        def send(side, h, to):
+            n = side * 2 + h
+            copy(half_of(s_nb.at[i, side], h), half_of(r_nb.at[i, side], h), nb_s.at[i, n], nb_r.at[i, n], to, leaf).start()
+
+        s_nb[i, 0, 256:512, :] = density(i, x_next, 1).astype(BF)
+        send(0, 1, p_next)
+        s_nb[i, 1, 0:256, :] = density(i, x_prev, 0).astype(BF)
+        send(1, 0, p_prev)
+        mine = density(i, x_next, 0)
+        arrived(r_opp.at[i, 0], op_r.at[i, 0])
+        s_nb[i, 0, 0:256, :] = (mine + r_opp[i, 0].astype(F32)).astype(BF)
+        send(0, 0, p_next)
+        mine = density(i, x_prev, 1)
+        arrived(r_opp.at[i, 1], op_r.at[i, 1])
+        s_nb[i, 1, 256:512, :] = (mine + r_opp[i, 1].astype(F32)).astype(BF)
+        send(1, 1, p_prev)
+
+    def own_part(i):
+        for h in range(2):
+            own[i, h * 256 : h * 256 + 256, :] = density(i, x, h)
+
+    def along_z(i):
+        for n in (1, 2, 0, 3):
+            arrived(half_of(r_nb.at[i, n // 2], n % 2), nb_r.at[i, n])
+
+        def summed(to):
+            rows = pl.ds(pl.multiple_of(to * 128, 128), 128)
+            return own[i, rows, :] + r_nb[i, 0, rows, :].astype(F32) + r_nb[i, 1, rows, :].astype(F32)
+
+        for t in (2, 1, 3):
+            to = (zh + t) % 4
+            sz[i, to] = summed(to).astype(BF)
+            copy(sz.at[i, to], rz.at[i, zh], z_s.at[i, t - 1], z_r.at[i, zh], x * 4 + to, leaf).start()
+        keep[i] = summed(zh)
+
+    def result(i):
+        total = keep[i]
+        for t in (1, 3, 2):
+            z_from = (zh + t) % 4
+            arrived(rz.at[i, z_from], z_r.at[i, z_from])
+            total = total + rz[i, z_from].astype(F32)
+        return total
+
+    opposite(0)
+    neighbours(0)
+    own_part(0)
 
     g_relay(3)
-    for i in range(4):
-        arrived(g_block(i, 1 - k), gc_r.at[i])
-    loads[6].wait()
-    loads[7].wait()
-
-    for t in range(1, 5):
-        x_to = (x + t) % 4
-
-        def g_rows(i, carry, x_to=x_to):
-            at = pl.multiple_of(i * 256, 256)
-            rows = pl.ds(pl.multiple_of(x_to * 512 + i * 256, 256), 256)
-            sx_g[x_to, pl.ds(at, 256), :] = density(mm(ftg[rows, :], rhs_g[...]), dg_v[rows, :], 256)
-            return carry
-
-        lax.fori_loop(0, 2, g_rows, 0)
-        if t < 4:
-            copy(sx_g.at[x_to], rx_g.at[x], xg_s.at[t - 1], xg_r.at[x], x_to * 4 + zh, leaf).start()
-
-    def along_z(sx, rx, sz, rz, xr, zs, zr):
-        for t in range(1, 4):
-            x_from = (x + t) % 4
-            arrived(rx.at[x_from], xr.at[x_from])
-        for t in range(1, 5):
-            to = (zh + t) % 4
-            rows = pl.ds(pl.multiple_of(to * 128, 128), 128)
-            total = sx[x, rows, :].astype(F32)
-            for u in range(1, 4):
-                total = total + rx[(x + u) % 4, rows, :].astype(F32)
-            if t < 4:
-                sz[to] = total.astype(BF)
-                copy(sz.at[to], rz.at[zh], zs.at[t - 1], zr.at[zh], x * 4 + to, leaf).start()
-        return total
-
-    own_cs = along_z(sx_c, rx_c, sz_c, rz_c, xc_r, zc_s, zc_r)
-    own_gs = along_z(sx_g, rx_g, sz_g, rz_g, xg_r, zg_s, zg_r)
-    for t in range(1, 4):
-        z_from = (zh + t) % 4
-        arrived(rz_c.at[z_from], zc_r.at[z_from])
-        own_cs = own_cs + rz_c[z_from].astype(F32)
-    out_c[...] = own_cs
-    for t in range(1, 4):
-        z_from = (zh + t) % 4
-        arrived(rz_g.at[z_from], zg_r.at[z_from])
-        own_gs = own_gs + rz_g[z_from].astype(F32)
-    out_g[...] = own_gs
+    g_finish()
+    for i in (6, 7, 11, 12):
+        loads[i].wait()
+    opposite(1)
+    opposite(2)
+    along_z(0)
+    neighbours(1)
+    neighbours(2)
+    own_part(1)
+    along_z(1)
+    own_part(2)
+    along_z(2)
+    out_c[...] = result(0)
+    out_g[:, 0:128] = result(1)
+    out_g[:, 128:256] = result(2)
 
     for t in range(3):
         sent(t_send.at[0], ty_s.at[t])
-        sent(sx_c.at[0], xc_s.at[t])
-        sent(sx_g.at[0], xg_s.at[t])
-        sent(sz_c.at[0], zc_s.at[t])
-        sent(sz_g.at[0], zg_s.at[t])
+        for i in range(3):
+            sent(sz.at[0, 0], z_s.at[i, t])
+    for i in range(3):
+        for h in range(2):
+            sent(s_opp.at[0, 0], op_s.at[i, h])
+        for n in range(4):
+            sent(s_opp.at[0, 0], nb_s.at[i, n])
     sent(d_send, dy_s.at[0])
     for t in range(7):
         sent(piece(part, 0), e3_s.at[t])
@@ -562,11 +606,13 @@
     vm = pltpu.VMEM
     dma = pltpu.SemaphoreType.DMA
     scratch = [
+        vm((2, 192), jnp.int32),
+        vm((4, 192), jnp.int32),
+        pltpu.SMEM((1, 2), F32),
         vm((128, 2048), BF),
         vm((2, 192, 128), BF),
         vm((2, 192, 256), BF),
-        vm((2048, 256), BF),
-        vm((2048, 512), BF),
+        vm((3, 2048, 256), BF),
         vm((2048, 384), BF),
         vm((2048, 384), BF),
         vm((2048, 512), BF),
@@ -580,17 +626,16 @@
         vm((768, 128), BF),
         vm((192, 384), BF),
         vm((192, 384), BF),
-        vm((384, 256), BF),
-        vm((384, 512), BF),
-        vm((4, 512, 128), BF),
-        vm((4, 512, 256), BF),
-        vm((4, 512, 128), BF),
-        vm((4, 512, 256), BF),
-        vm((4, 128, 128), BF),
-        vm((4, 128, 256), BF),
-        vm((4, 128, 128), BF),
-        vm((4, 128, 256), BF),
-        dma((8,)),
+        vm((3, 384, 256), BF),
+        vm((3, 2, 256, 128), BF),
+        vm((3, 2, 256, 128), BF),
+        vm((3, 2, 512, 128), BF),
+        vm((3, 2, 512, 128), BF),
+        vm((3, 512, 128), F32),
+        vm((3, 4, 128, 128), BF),
+        vm((3, 4, 128, 128), BF),
+        vm((3, 128, 128), F32),
+        dma((13,)),
         dma((3,)),
         dma((4,)),
         dma((1,)),
@@ -609,16 +654,14 @@
         dma((4,)),
         dma((4,)),
         dma((4,)),
-        dma((3,)),
-        dma((4,)),
-        dma((3,)),
-        dma((4,)),
-        dma((3,)),
-        dma((4,)),
-        dma((3,)),
-        dma((4,)),
+        dma((3, 2)),
+        dma((3, 2)),
+        dma((3, 4)),
+        dma((3, 4)),
+        dma((3, 3)),
+        dma((3, 4)),
     ]
-    any_spec = pl.BlockSpec(memory_space=pl.ANY)
+    hbm = pl.BlockSpec(memory_space=pltpu.HBM)
     vm_spec = pl.BlockSpec(memory_space=pltpu.VMEM)
     return pl.pallas_call(
         kernel,
@@ -626,11 +669,11 @@
             jax.ShapeDtypeStruct((128, 128), F32),
             jax.ShapeDtypeStruct((128, 256), F32),
         ],
-        in_specs=[any_spec] * 5 + [vm_spec] * 2 + [pl.BlockSpec(memory_space=pltpu.SMEM)],
+        in_specs=[hbm] * 8,
         out_specs=[vm_spec, vm_spec],
         scratch_shapes=scratch,
         compiler_params=pltpu.CompilerParams(
-            collective_id=0, has_side_effects=True, vmem_limit_bytes=40 * 1024 * 1024
+            collective_id=0, has_side_effects=True, vmem_limit_bytes=60 * 1024 * 1024
         ),
         cost_estimate=pl.CostEstimate(flops=3_000_000_000, bytes_accessed=5_000_000, transcendentals=0),
     )(*args)

time: 87.2 us -> 74.9 us (0.86)
  Pallas kernels: 77.2 us -> 70.3 us
  local copies, waits for them, and re-layouts: 8.98 us -> 3.04 us
    pallas_call x1, Pallas kernels: 77.2 us -> 70.3 us  [local(): pl.pallas_call(kernel, out_shape=[jax.ShapeDtypeStruct((128, 128), F32),...]
    unnamed x18 -> x2, local copies, waits for them, and re-layouts: 8.98 us -> 3.04 us
where the time goes in v2:
time: 74.9 us; the launch traced here: 74 us
  Pallas kernels  70.3 us (94%)
  local copies, waits for them, and re-layouts  3.04 us (4%)
    pallas_call x1, Pallas kernels, local(): pl.pallas_call(kernel, out_shape=[jax.ShapeDtypeStruct((128, 128), F32),...  70.3 us
    unnamed x2, local copies, waits for them, and re-layouts  3.04 us

profile of v2, /device:TPU:1, one launch (start us, length us, event | category | flops | bytes accessed | tf_op | source)
XLA Modules:
  0.0 74.0 jit_solution(4991742988381747848)
XLA Ops:
  0.6 70.3 %shard_map.95 = (f32[128,128]{1,0:T(8,128)}, f32[128,256]{1,0:T(8,128)}) custom-call(bf16[1,2,64,2048]{3,2,1,0:T(8,128)(2,1)} %root.1, bf16[1,2,192,128]{3,2,1,0:T(8,128)(2,1)} %fc.1, bf16[1,2,192,256]{3,2,1,0:T(8,128)(2,1)} %fg.1, bf16[1,2,2048,128]{3,2,1,0:T(8,128)(2,1)} %dc.1, bf16[1,2,2048,256]{3,2,1,0:T(8,128)(2,1)} %dg.1, s32[2,192]{1,0:T(2,128)} %sc_hbm.1, ...), custom_call_target="tpu_custom_call" | custom-call | flops 3000000000 | bytes 5000000 | tf_op jit(solution)/shard_map/pallas_call | solution.py:666
  70.9 1.5 %copy.12 = f32[128,128]{1,0:T(8,128)} copy(f32[128,128]{1,0:T(8,128)} %get-tuple-element.4) | data formatting | bytes 131072
  72.4 1.6 %copy.13 = f32[128,256]{1,0:T(8,128)} copy(f32[128,256]{1,0:T(8,128)} %get-tuple-element.5) | data formatting | bytes 262144

commit v3 on v2

--- a/solution.py
+++ b/solution.py
@@ -83,16 +83,17 @@
     d_send,
     d_recv,
     part,
+    sw_recv,
+    half,
     rs_recv,
     full,
     acat,
     agcat,
     rhs,
-    s_opp,
+    s_out,
     r_opp,
-    s_nb,
     r_nb,
-    own,
+    dens,
     sz,
     rz,
     keep,
@@ -101,10 +102,14 @@
     ty_r,
     dy_s,
     dy_r,
+    sw_s,
+    sw_r,
     e3_s,
     e3_r,
     e4_s,
     e4_r,
+    e5_s,
+    e5_r,
     cz_s,
     cz_r,
     cy_s,
@@ -121,6 +126,7 @@
     nb_r,
     z_s,
     z_r,
+    across,
 ):
     p = lax.axis_index("pole")
     leaf = lax.axis_index("leaf")
@@ -156,12 +162,16 @@
     def greet(pole_to, leaf_to):
         pl.semaphore_signal(barrier, inc=1, device_id=(pole_to, leaf_to), device_id_type=MESH)
 
+    mate = base + e + 1 - 2 * k
+    for t in (1, 3):
+        greet(x * 4 + (zh + t) % 4, leaf)
+    for t in (2, 1, 3):
+        greet(p, (y + t) % 4 * 8 + e)
     for t in range(1, 4):
-        greet(p, (y + t) % 4 * 8 + e)
-        greet((x + t) % 4 * 4 + zh, leaf)
-        greet(x * 4 + (zh + t) % 4, leaf)
-    for t in range(1, 8):
-        greet(p, base + (e + t) % 8)
+        greet(p, base + (e + 2 * t) % 8)
+    greet((x + 1) % 4 * 4 + zh, leaf)
+    greet((x + 3) % 4 * 4 + zh, leaf)
+    greet(p, mate)
 
     loads = [
         pltpu.make_async_copy(root.at[0, 0], root_v.at[0:64], lsem.at[0]),
@@ -214,7 +224,11 @@
             low_lanes, taken[0:64, at + 128 : at + 256], taken[64:128, at + 128 : at + 256]
         ).astype(BF)
 
-    pl.semaphore_wait(barrier, 16)
+    pl.semaphore_wait(barrier, 11)
+    for t in (1, 3):
+        pl.semaphore_signal(
+            across, inc=1, device_id=(x * 4 + (zh + t) % 4, leaf), device_id_type=MESH
+        )
 
     for t in range(1, 4):
         y_to = (y + t) % 4
@@ -224,8 +238,8 @@
     def c_block(yy, j, kk):
         return ftc.at[pl.ds(pl.multiple_of((yy * 8 + j * 2 + kk) * 128, 128), 128)]
 
-    def g_block(j, kk):
-        return ftg.at[pl.ds(pl.multiple_of((j * 2 + kk) * 256, 256), 256)]
+    def g_block(j, kk, part_at):
+        return ftg.at[pl.ds(pl.multiple_of((j * 2 + kk) * 256 + part_at * 128, 128), 128)]
 
     def c_up(j):
         return copy(c_block(yp, j, k), c_block(yp, j, k), cz_s.at[j], cz_r.at[j], p, base + e + 2)
@@ -240,14 +254,14 @@
         i = yy * 4 + j
         return copy(c_block(yy, j, k), c_block(yy, j, k), cc_s.at[i], cc_r.at[i], p, base + e + 1 - 2 * k)
 
-    def g_up(j):
-        return copy(g_block(j, k), g_block(j, k), gz_s.at[j], gz_r.at[j], p, base + e + 2)
-
-    def g_down(j):
-        return copy(g_block(j, k), g_block(j, k), gz_s.at[4 + j], gz_r.at[j], p, base + e - 2)
-
-    def g_core(j):
-        return copy(g_block(j, k), g_block(j, k), gc_s.at[j], gc_r.at[j], p, base + e + 1 - 2 * k)
+    def g_up(j, b):
+        return copy(g_block(j, k, b), g_block(j, k, b), gz_s.at[0, b, j], gz_r.at[b, j], p, base + e + 2)
+
+    def g_down(j, b):
+        return copy(g_block(j, k, b), g_block(j, k, b), gz_s.at[1, b, j], gz_r.at[b, j], p, base + e - 2)
+
+    def g_core(j, b):
+        return copy(g_block(j, k, b), g_block(j, k, b), gc_s.at[b, j], gc_r.at[b, j], p, mate)
 
     def c_first():
         @pl.when(zl < 3)
@@ -258,19 +272,18 @@
         def _():
             c_down(zl).start()
 
-        c_side(zl).start()
         c_core(yp, zl).start()
 
-    def g_first():
+    def g_first(b):
         @pl.when(zl < 3)
         def _():
-            g_up(zl).start()
+            g_up(zl, b).start()
 
         @pl.when(zl > 0)
         def _():
-            g_down(zl).start()
-
-        g_core(zl).start()
+            g_down(zl, b).start()
+
+        g_core(zl, b).start()
 
     def c_relay(s):
         @pl.when(zl >= s)
@@ -297,28 +310,28 @@
             c_side(j).start()
             c_core(yp, j).start()
 
-    def g_relay(s):
+    def g_relay(s, b):
         @pl.when(zl >= s)
         def _():
             j = zl - s
-            arrived(g_block(j, k), gz_r.at[j])
+            arrived(g_block(j, k, b), gz_r.at[b, j])
 
             @pl.when(zl < 3)
             def _():
-                g_up(j).start()
-
-            g_core(j).start()
+                g_up(j, b).start()
+
+            g_core(j, b).start()
 
         @pl.when(zl + s <= 3)
         def _():
             j = zl + s
-            arrived(g_block(j, k), gz_r.at[j])
+            arrived(g_block(j, k, b), gz_r.at[b, j])
 
             @pl.when(zl > 0)
             def _():
-                g_down(j).start()
-
-            g_core(j).start()
+                g_down(j, b).start()
+
+            g_core(j, b).start()
 
     def c_finish():
         for i in range(4):
@@ -327,12 +340,9 @@
         for i in range(8):
             arrived(c_block(i // 4, i % 4, 1 - k), cc_r.at[i])
 
-    def g_finish():
-        for i in range(4):
-            arrived(g_block(i, 1 - k), gc_r.at[i])
-
     c_first()
-    g_first()
+    g_first(0)
+    g_first(1)
 
     col0 = column(row_of(sg, y, slice(0, 128)))
     col1 = column(twice(row_of(sg, y, slice(128, 192))))
@@ -369,6 +379,7 @@
         ],
         axis=0,
     )
+    c_relay(1)
     for t in range(1, 4):
         y_from = (y + t) % 4
         arrived(t_recv.at[y_from], ty_r.at[y_from])
@@ -379,31 +390,52 @@
     part[576:672, :] = (d_re + d_recv[0:96, :].astype(F32)).astype(BF)
     part[672:768, :] = (d_im + d_recv[96:192, :].astype(F32)).astype(BF)
 
+    c_side(zl).start()
+
     def piece(ref, i):
         return ref.at[pl.ds(pl.multiple_of(i * 96, 96), 96)]
 
-    for t in range(1, 8):
-        to = (e + t) % 8
-        copy(piece(part, to), rs_recv.at[e], e3_s.at[t - 1], e3_r.at[e], p, base + to).start()
-    c_relay(1)
-    total = part[pl.ds(pl.multiple_of(e * 96, 96), 96), :].astype(F32)
-    for t in range(1, 8):
-        at = (e + t) % 8
+    def side_rows(kk):
+        return pl.ds(pl.multiple_of(kk * 384, 128), 384)
+
+    swap = copy(part.at[side_rows(1 - k)], sw_recv, sw_s.at[0], sw_r.at[0], p, mate)
+    swap.start()
+    arrived(sw_recv, sw_r.at[0])
+    half[...] = (part[side_rows(k), :].astype(F32) + sw_recv[...].astype(F32)).astype(BF)
+
+    for t in (2, 1, 3):
+        to = (zl + t) % 4
+        copy(piece(half, to), rs_recv.at[zl], e3_s.at[t - 1], e3_r.at[zl], p, base + to * 2 + k).start()
+    c_relay(2)
+    total = half[pl.ds(pl.multiple_of(zl * 96, 96), 96), :].astype(F32)
+    for t in (1, 3, 2):
+        at = (zl + t) % 4
         arrived(rs_recv.at[at], e3_r.at[at])
         total = total + rs_recv[at].astype(F32)
-    full[pl.ds(pl.multiple_of(e * 96, 96), 96), :] = total.astype(BF)
-
-    for t in range(1, 8):
-        to = (e + t) % 8
-        copy(piece(full, e), piece(full, e), e4_s.at[t - 1], e4_r.at[e], p, base + to).start()
-    c_relay(2)
-    g_relay(1)
-    for t in range(1, 8):
-        at = (e + t) % 8
-        arrived(piece(full, at), e4_r.at[at])
+    mine = k * 4 + zl
+    full[pl.ds(pl.multiple_of(mine * 96, 96), 96), :] = total.astype(BF)
+
+    for t in (2, 1, 3):
+        to = (zl + t) % 4
+        copy(piece(full, mine), piece(full, mine), e4_s.at[t - 1], e4_r.at[zl], p, base + to * 2 + k).start()
+
+    def to_mate(at):
+        i = k * 4 + at
+        copy(piece(full, i), piece(full, i), e5_s.at[at], e5_r.at[at], p, mate).start()
+
+    to_mate(zl)
+    c_relay(3)
+    for t in (1, 3, 2):
+        at = (zl + t) % 4
+        arrived(piece(full, k * 4 + at), e4_r.at[at])
+        to_mate(at)
+    for at in range(4):
+        arrived(piece(full, (1 - k) * 4 + at), e5_r.at[at])
     for b in range(3):
         acat[:, b * 128 : b * 128 + 128] = full[b * 192 : b * 192 + 192, :]
 
+    g_relay(1, 0)
+    g_relay(1, 1)
     g_re, g_im = right_side(fc_v[0], fc_v[1])
     a_now = acat[...]
     off_re = (-mm(a_now, g_re)).astype(BF)
@@ -412,8 +444,98 @@
     rhs[0, :, 0:128] = r_re
     rhs[0, :, 128:256] = r_im
 
-    c_relay(3)
     c_finish()
+
+    w_im = pw[0, 0]
+    w_re = pw[0, 1]
+    x_next = (x + 1) % 4
+    x_prev = (x + 3) % 4
+    p_next = x_next * 4 + zh
+    p_prev = x_prev * 4 + zh
+
+    def process(i, quarter, role, b):
+        at = b * 128
+        ft_ref = ftc if i == 0 else ftg
+        rows = [pl.ds(pl.multiple_of(quarter * 512 + h * 256 + at, 128), 128) for h in range(2)]
+        ft = jnp.concatenate([ft_ref[r, :] for r in rows], axis=0)
+        reduced = mm(ft, rhs[i])
+        here = pl.ds(at, 128)
+        for h in range(2):
+            inverse = diag_v[i, rows[h], :].astype(F32) - reduced[h * 128 : h * 128 + 128]
+            inverse = inverse.astype(BF).astype(F32)
+            value = w_im * inverse[:, 128:256] + w_re * inverse[:, 0:128]
+            dens[i, role, h, here] = value
+            s_out[i, role, h, here] = value.astype(BF)
+
+        @pl.when(role == 2)
+        def _():
+            opp_copy(i, 0, b, p_next).start()
+            opp_copy(i, 1, b, p_prev).start()
+
+        @pl.when(role == 1)
+        def _():
+            nb_copy(i, 0, 1, b).start()
+
+        @pl.when(role == 3)
+        def _():
+            nb_copy(i, 1, 0, b).start()
+
+    def opp_copy(i, h, b, to):
+        here = pl.ds(b * 128, 128)
+        return copy(s_out.at[i, 2, h, here], r_opp.at[i, h, here], op_s.at[i, h, b], op_r.at[i, h, b], to, leaf)
+
+    def nb_copy(i, side, h, b):
+        here = pl.ds(b * 128, 128)
+        return copy(
+            s_out.at[i, 1 + 2 * side, h, here],
+            r_nb.at[i, side, h, here],
+            nb_s.at[i, side, h, b],
+            nb_r.at[i, side, h, b],
+            p_prev if side else p_next,
+            leaf,
+        )
+
+    def complete(i, b):
+        here = pl.ds(b * 128, 128)
+        for side in range(2):
+            arrived(r_opp.at[i, side, here], op_r.at[i, side, b])
+            s_out[i, 1 + 2 * side, side, here] = (
+                dens[i, 1 + 2 * side, side, here] + r_opp[i, side, here].astype(F32)
+            ).astype(BF)
+            nb_copy(i, side, side, b).start()
+
+    def z_copy(i, to):
+        return copy(sz.at[i, to], rz.at[i, zh], z_s.at[i, to], z_r.at[i, zh], x * 4 + to, leaf)
+
+    def along_z(i, b):
+        here = pl.ds(b * 128, 128)
+        for h in range(2):
+            for side in range(2):
+                arrived(r_nb.at[i, side, h, here], nb_r.at[i, side, h, b])
+        for h in range(2):
+            to = 2 * h + b
+            total = dens[i, 0, h, here] + r_nb[i, 0, h, here].astype(F32) + r_nb[i, 1, h, here].astype(F32)
+
+            @pl.when(zh != to)
+            def _():
+                sz[i, to] = total.astype(BF)
+                z_copy(i, to).start()
+
+            @pl.when(zh == to)
+            def _():
+                keep[i] = total
+
+    def result(i):
+        total = keep[i]
+        for t in (1, 3, 2):
+            z_from = (zh + t) % 4
+            arrived(rz.at[i, z_from], z_r.at[i, z_from])
+            total = total + rz[i, z_from].astype(F32)
+        return total
+
+    for b in range(2):
+        for r in (2, 1, 3, 0):
+            process(0, (x + r) % 4, r, b)
 
     ft_r = mm(rl[0:128, :], ftc[...])
     lane384 = lax.broadcasted_iota(jnp.int32, (128, 384), 1)
@@ -471,8 +593,9 @@
     ).astype(BF)
     agcat[:, 256:384] = ag[:, 256:384].astype(BF)
 
-    g_relay(2)
-
+
+    g_relay(2, 0)
+    g_relay(2, 1)
     gg_re, gg_im = right_side(fg_v[0], fg_v[1])
     ag_now = agcat[...]
     goff_re = (-mm(ag_now, gg_re)).astype(BF)
@@ -482,124 +605,79 @@
         rhs[1 + h, :, 0:128] = r_re[:, h * 128 : h * 128 + 128]
         rhs[1 + h, :, 128:256] = r_im[:, h * 128 : h * 128 + 128]
 
-    w_im = pw[0, 0]
-    w_re = pw[0, 1]
-
-    def density(i, quarter, half):
-        rows = pl.ds(pl.multiple_of(quarter * 512 + half * 256, 256), 256)
-        ft = ftc[rows, :] if i == 0 else ftg[rows, :]
-        rest_of = diag_v[i, rows, :].astype(F32) - mm(ft, rhs[i])
-        rest_of = rest_of.astype(BF).astype(F32)
-        return w_im * rest_of[:, 128:256] + w_re * rest_of[:, 0:128]
-
-    x_next = (x + 1) % 4
-    x_prev = (x + 3) % 4
-    x_far = (x + 2) % 4
-    p_next = x_next * 4 + zh
-    p_prev = x_prev * 4 + zh
-
-    def half_of(ref, h):
-        return ref.at[pl.ds(h * 256, 256)]
-
-    def opposite(i):
-        for h, to in ((0, p_next), (1, p_prev)):
-            s_opp[i, h] = density(i, x_far, h).astype(BF)
-            copy(s_opp.at[i, h], r_opp.at[i, h], op_s.at[i, h], op_r.at[i, h], to, leaf).start()
-
-    def neighbours(i):
-        def send(side, h, to):
-            n = side * 2 + h
-            copy(half_of(s_nb.at[i, side], h), half_of(r_nb.at[i, side], h), nb_s.at[i, n], nb_r.at[i, n], to, leaf).start()
-
-        s_nb[i, 0, 256:512, :] = density(i, x_next, 1).astype(BF)
-        send(0, 1, p_next)
-        s_nb[i, 1, 0:256, :] = density(i, x_prev, 0).astype(BF)
-        send(1, 0, p_prev)
-        mine = density(i, x_next, 0)
-        arrived(r_opp.at[i, 0], op_r.at[i, 0])
-        s_nb[i, 0, 0:256, :] = (mine + r_opp[i, 0].astype(F32)).astype(BF)
-        send(0, 0, p_next)
-        mine = density(i, x_prev, 1)
-        arrived(r_opp.at[i, 1], op_r.at[i, 1])
-        s_nb[i, 1, 256:512, :] = (mine + r_opp[i, 1].astype(F32)).astype(BF)
-        send(1, 1, p_prev)
-
-    def own_part(i):
-        for h in range(2):
-            own[i, h * 256 : h * 256 + 256, :] = density(i, x, h)
-
-    def along_z(i):
-        for n in (1, 2, 0, 3):
-            arrived(half_of(r_nb.at[i, n // 2], n % 2), nb_r.at[i, n])
-
-        def summed(to):
-            rows = pl.ds(pl.multiple_of(to * 128, 128), 128)
-            return own[i, rows, :] + r_nb[i, 0, rows, :].astype(F32) + r_nb[i, 1, rows, :].astype(F32)
-
-        for t in (2, 1, 3):
-            to = (zh + t) % 4
-            sz[i, to] = summed(to).astype(BF)
-            copy(sz.at[i, to], rz.at[i, zh], z_s.at[i, t - 1], z_r.at[i, zh], x * 4 + to, leaf).start()
-        keep[i] = summed(zh)
-
-    def result(i):
-        total = keep[i]
-        for t in (1, 3, 2):
-            z_from = (zh + t) % 4
-            arrived(rz.at[i, z_from], z_r.at[i, z_from])
-            total = total + rz[i, z_from].astype(F32)
-        return total
-
-    opposite(0)
-    neighbours(0)
-    own_part(0)
-
-    g_relay(3)
-    g_finish()
+    def g_quarter(q, b):
+        arrived(g_block(q, 1 - k, b), gc_r.at[b, q])
+        role = (q - x + 4) % 4
+        process(1, q, role, b)
+        process(2, q, role, b)
+
     for i in (6, 7, 11, 12):
         loads[i].wait()
-    opposite(1)
-    opposite(2)
-    along_z(0)
-    neighbours(1)
-    neighbours(2)
-    own_part(1)
-    along_z(1)
-    own_part(2)
-    along_z(2)
+    pl.semaphore_wait(across, 2)
+    far = 3 * (1 - zl // 2)
+    for b in range(2):
+        g_quarter(zl, b)
+    for b in range(2):
+        complete(0, b)
+    for b in range(2):
+        g_quarter(zl + 1 - 2 * (zl // 2), b)
+    for b in range(2):
+        g_quarter((3 * zl + 2) % 5, b)
+    for b in range(2):
+        along_z(0, b)
+    for b in range(2):
+        g_relay(3, b)
+        g_quarter(far, b)
+    for b in range(2):
+        for i in (1, 2):
+            complete(i, b)
+    for b in range(2):
+        for i in (1, 2):
+            along_z(i, b)
     out_c[...] = result(0)
     out_g[:, 0:128] = result(1)
     out_g[:, 128:256] = result(2)
 
     for t in range(3):
         sent(t_send.at[0], ty_s.at[t])
-        for i in range(3):
-            sent(sz.at[0, 0], z_s.at[i, t])
     for i in range(3):
-        for h in range(2):
-            sent(s_opp.at[0, 0], op_s.at[i, h])
-        for n in range(4):
-            sent(s_opp.at[0, 0], nb_s.at[i, n])
+        for to in range(4):
+
+            @pl.when(zh != to)
+            def _(i=i, to=to):
+                sent(sz.at[0, 0], z_s.at[i, to])
+
+        for b in range(2):
+            for h in range(2):
+                sent(sz.at[0, 0], op_s.at[i, h, b])
+                for side in range(2):
+                    sent(sz.at[0, 0], nb_s.at[i, side, h, b])
     sent(d_send, dy_s.at[0])
-    for t in range(7):
-        sent(piece(part, 0), e3_s.at[t])
+    sent(sw_recv, sw_s.at[0])
+    for t in range(3):
+        sent(piece(half, 0), e3_s.at[t])
         sent(piece(full, 0), e4_s.at[t])
+    for t in range(4):
+        sent(piece(full, 0), e5_s.at[t])
     for j in range(4):
 
         @pl.when((zl < 3) & (j <= zl))
         def _(j=j):
             sent(c_block(0, 0, 0), cz_s.at[j])
-            sent(g_block(0, 0), gz_s.at[j])
+            for b in range(2):
+                sent(g_block(0, 0, 0), gz_s.at[0, b, j])
 
         @pl.when((zl > 0) & (j >= zl))
         def _(j=j):
             sent(c_block(0, 0, 0), cz_s.at[4 + j])
-            sent(g_block(0, 0), gz_s.at[4 + j])
+            for b in range(2):
+                sent(g_block(0, 0, 0), gz_s.at[1, b, j])
 
         sent(c_block(0, 0, 0), cy_s.at[j])
         sent(c_block(0, 0, 0), cc_s.at[j])
         sent(c_block(0, 0, 0), cc_s.at[4 + j])
-        sent(g_block(0, 0), gc_s.at[j])
+        for b in range(2):
+            sent(g_block(0, 0, 0), gc_s.at[b, j])
 
 
 def local(*args):
@@ -622,16 +700,17 @@
         vm((192, 128), BF),
         vm((192, 128), BF),
         vm((768, 128), BF),
-        vm((8, 96, 128), BF),
+        vm((384, 128), BF),
+        vm((384, 128), BF),
+        vm((4, 96, 128), BF),
         vm((768, 128), BF),
         vm((192, 384), BF),
         vm((192, 384), BF),
         vm((3, 384, 256), BF),
+        vm((3, 4, 2, 256, 128), BF),
         vm((3, 2, 256, 128), BF),
-        vm((3, 2, 256, 128), BF),
-        vm((3, 2, 512, 128), BF),
-        vm((3, 2, 512, 128), BF),
-        vm((3, 512, 128), F32),
+        vm((3, 2, 2, 256, 128), BF),
+        vm((3, 4, 2, 256, 128), F32),
         vm((3, 4, 128, 128), BF),
         vm((3, 4, 128, 128), BF),
         vm((3, 128, 128), F32),
@@ -640,26 +719,31 @@
         dma((4,)),
         dma((1,)),
         dma((1,)),
-        dma((7,)),
-        dma((8,)),
-        dma((7,)),
-        dma((8,)),
+        dma((1,)),
+        dma((1,)),
+        dma((3,)),
+        dma((4,)),
+        dma((3,)),
+        dma((4,)),
+        dma((4,)),
+        dma((4,)),
         dma((8,)),
         dma((4,)),
         dma((4,)),
         dma((4,)),
         dma((8,)),
         dma((8,)),
-        dma((8,)),
-        dma((4,)),
-        dma((4,)),
-        dma((4,)),
-        dma((3, 2)),
-        dma((3, 2)),
+        dma((2, 2, 4)),
+        dma((2, 4)),
+        dma((2, 4)),
+        dma((2, 4)),
+        dma((3, 2, 2)),
+        dma((3, 2, 2)),
+        dma((3, 2, 2, 2)),
+        dma((3, 2, 2, 2)),
         dma((3, 4)),
         dma((3, 4)),
-        dma((3, 3)),
-        dma((3, 4)),
+        pltpu.SemaphoreType.REGULAR,
     ]
     hbm = pl.BlockSpec(memory_space=pltpu.HBM)
     vm_spec = pl.BlockSpec(memory_space=pltpu.VMEM)

time: 74.9 us -> 70.4 us (0.940)
  Pallas kernels: 70.3 us -> 65.5 us
    pallas_call x1, Pallas kernels: 70.3 us -> 65.5 us  [local(): pl.pallas_call(kernel, out_shape=[jax.ShapeDtypeStruct((128, 128), F32),...]
where the time goes in v3:
time: 70.4 us; the launch traced here: 69.1 us
  Pallas kernels  65.5 us (93%)
  local copies, waits for them, and re-layouts  3.04 us (4%)
    pallas_call x1, Pallas kernels, local(): pl.pallas_call(kernel, out_shape=[jax.ShapeDtypeStruct((128, 128), F32),...  65.5 us
    unnamed x2, local copies, waits for them, and re-layouts  3.04 us

profile of v3, /device:TPU:1, one launch (start us, length us, event | category | flops | bytes accessed | tf_op | source)
XLA Modules:
  0.0 69.1 jit_solution(16318110860791551569)
XLA Ops:
  0.6 65.5 %shard_map.95 = (f32[128,128]{1,0:T(8,128)}, f32[128,256]{1,0:T(8,128)}) custom-call(bf16[1,2,64,2048]{3,2,1,0:T(8,128)(2,1)} %root.1, bf16[1,2,192,128]{3,2,1,0:T(8,128)(2,1)} %fc.1, bf16[1,2,192,256]{3,2,1,0:T(8,128)(2,1)} %fg.1, bf16[1,2,2048,128]{3,2,1,0:T(8,128)(2,1)} %dc.1, bf16[1,2,2048,256]{3,2,1,0:T(8,128)(2,1)} %dg.1, s32[2,192]{1,0:T(2,128)} %sc_hbm.1, ...), custom_call_target="tpu_custom_call" | custom-call | flops 3000000000 | bytes 5000000 | tf_op jit(solution)/shard_map/pallas_call | solution.py:750
  66.1 1.5 %copy.12 = f32[128,128]{1,0:T(8,128)} copy(f32[128,128]{1,0:T(8,128)} %get-tuple-element.4) | data formatting | bytes 131072
  67.6 1.6 %copy.13 = f32[128,256]{1,0:T(8,128)} copy(f32[128,256]{1,0:T(8,128)} %get-tuple-element.5) | data formatting | bytes 262144

commit v4 on v3

--- a/solution.py
+++ b/solution.py
@@ -342,7 +342,6 @@
 
     c_first()
     g_first(0)
-    g_first(1)
 
     col0 = column(row_of(sg, y, slice(0, 128)))
     col1 = column(twice(row_of(sg, y, slice(128, 192))))
@@ -424,6 +423,7 @@
         copy(piece(full, i), piece(full, i), e5_s.at[at], e5_r.at[at], p, mate).start()
 
     to_mate(zl)
+    g_first(1)
     c_relay(3)
     for t in (1, 3, 2):
         at = (zl + t) % 4
@@ -750,8 +750,8 @@
     return pl.pallas_call(
         kernel,
         out_shape=[
-            jax.ShapeDtypeStruct((128, 128), F32),
-            jax.ShapeDtypeStruct((128, 256), F32),
+            pltpu.VMEM((128, 128), F32),
+            pltpu.VMEM((128, 256), F32),
         ],
         in_specs=[hbm] * 8,
         out_specs=[vm_spec, vm_spec],

time: 70.4 us -> 66.6 us (0.946)
  the two profiles are of different devices: /device:TPU:1 before, /device:TPU:19 now
where the time goes in v4:
time: 66.6 us; the launch traced here: 66.5 us
  Pallas kernels  64.6 us (97%)
  local copies, waits for them, and re-layouts  1.29 us (2%)
    pallas_call x1, Pallas kernels, local(): pl.pallas_call(kernel, out_shape=[pltpu.VMEM((128, 128), F32), pltpu.VMEM...  64.6 us

profile of v4, /device:TPU:19, one launch (start us, length us, event | category | flops | bytes accessed | tf_op | source)
XLA Modules:
  0.0 66.5 jit_solution(6104850992002357273)
XLA Ops:
  0.6 64.6 %shard_map.95 = (f32[128,128]{1,0:T(8,128)S(1)}, f32[128,256]{1,0:T(8,128)S(1)}) custom-call(bf16[1,2,64,2048]{3,2,1,0:T(8,128)(2,1)} %root.1, bf16[1,2,192,128]{3,2,1,0:T(8,128)(2,1)} %fc.1, bf16[1,2,192,256]{3,2,1,0:T(8,128)(2,1)} %fg.1, bf16[1,2,2048,128]{3,2,1,0:T(8,128)(2,1)} %dc.1, bf16[1,2,2048,256]{3,2,1,0:T(8,128)(2,1)} %dg.1, s32[2,192]{1,0:T(2,128)} %sc_hbm.1, ...), custom_call_target="tpu_custom_call" | custom-call | flops 3000000000 | bytes 5000000 | tf_op jit(solution)/shard_map/pallas_call | solution.py:750
  65.2 0.6 copy.12
  65.9 0.7 copy.13

commit v5 on v4

--- a/solution.py
+++ b/solution.py
@@ -197,17 +197,17 @@
     ftc[pl.ds(own_c, 128), :] = transposed(fc_v, slice(0, 128))
     loads[3].wait()
     ftg[pl.ds(own_g, 128), :] = transposed(fg_v, slice(0, 128))
-    ftg[pl.ds(pl.multiple_of(own_g + 128, 128), 128), :] = transposed(fg_v, slice(128, 256))
 
     loads[8].wait()
     loads[9].wait()
     loads[10].wait()
-    child_rows = [sc[0:1, 0:128], twice(sc[0:1, 128:192]), sc[1:2, 0:128], twice(sc[1:2, 128:192])]
+    high = jnp.concatenate([sc[0:1, 128:192], sc[1:2, 128:192]], axis=1)
+    child_rows = [sc[0:1, 0:128], sc[1:2, 0:128], high]
     hot_rows = jnp.concatenate(child_rows, axis=1).astype(F32)
 
     def build_hot(i, carry):
         at = pl.multiple_of(i * 128, 128)
-        ids = iota((128, 512), 0) + (i * 128).astype(F32)
+        ids = iota((128, 384), 0) + (i * 128).astype(F32)
         oh[pl.ds(at, 128), :] = hot(ids == hot_rows)
         return carry
 
@@ -216,13 +216,14 @@
     loads[1].wait()
     taken = mm(root_v[...], oh[...])
     low_lanes = iota((64, 128), 1) < 64
+    high_re = taken[0:64, 256:384]
+    high_im = taken[64:128, 256:384]
     for ch in range(2):
-        at = ch * 256
+        at = ch * 128
         t_send[ch, 0:64, :] = taken[0:64, at : at + 128].astype(BF)
         t_send[ch, 64:128, :] = taken[64:128, at : at + 128].astype(BF)
-        t_send[ch, 128:192, :] = jnp.where(
-            low_lanes, taken[0:64, at + 128 : at + 256], taken[64:128, at + 128 : at + 256]
-        ).astype(BF)
+    t_send[0, 128:192, :] = jnp.where(low_lanes, high_re, pltpu.roll(high_im, 64, 1)).astype(BF)
+    t_send[1, 128:192, :] = jnp.where(low_lanes, pltpu.roll(high_re, 64, 1), high_im).astype(BF)
 
     pl.semaphore_wait(barrier, 11)
     for t in (1, 3):
@@ -342,6 +343,7 @@
 
     c_first()
     g_first(0)
+    ftg[pl.ds(pl.multiple_of(own_g + 128, 128), 128), :] = transposed(fg_v, slice(128, 256))
 
     col0 = column(row_of(sg, y, slice(0, 128)))
     col1 = column(twice(row_of(sg, y, slice(128, 192))))
@@ -634,19 +636,9 @@
     for b in range(2):
         for i in (1, 2):
             along_z(i, b)
-    out_c[...] = result(0)
-    out_g[:, 0:128] = result(1)
-    out_g[:, 128:256] = result(2)
-
     for t in range(3):
         sent(t_send.at[0], ty_s.at[t])
     for i in range(3):
-        for to in range(4):
-
-            @pl.when(zh != to)
-            def _(i=i, to=to):
-                sent(sz.at[0, 0], z_s.at[i, to])
-
         for b in range(2):
             for h in range(2):
                 sent(sz.at[0, 0], op_s.at[i, h, b])
@@ -679,6 +671,16 @@
         for b in range(2):
             sent(g_block(0, 0, 0), gc_s.at[b, j])
 
+    out_c[...] = result(0)
+    out_g[:, 0:128] = result(1)
+    out_g[:, 128:256] = result(2)
+    for i in range(3):
+        for to in range(4):
+
+            @pl.when(zh != to)
+            def _(i=i, to=to):
+                sent(sz.at[0, 0], z_s.at[i, to])
+
 
 def local(*args):
     vm = pltpu.VMEM
@@ -693,7 +695,7 @@
         vm((3, 2048, 256), BF),
         vm((2048, 384), BF),
         vm((2048, 384), BF),
-        vm((2048, 512), BF),
+        vm((2048, 384), BF),
         vm((256, 2048), BF),
         vm((2, 192, 128), BF),
         vm((4, 192, 128), BF),

time: 66.6 us -> 66.5 us (level)
  no operation moved by 1% of the time
where the time goes in v5:
time: 66.5 us; the launch traced here: 66.4 us
  Pallas kernels  64.5 us (97%)
  local copies, waits for them, and re-layouts  1.29 us (2%)
    pallas_call x1, Pallas kernels, local(): pl.pallas_call(kernel, out_shape=[pltpu.VMEM((128, 128), F32), pltpu.VMEM...  64.5 us

profile of v5, /device:TPU:19, one launch (start us, length us, event | category | flops | bytes accessed | tf_op | source)
XLA Modules:
  0.0 66.4 jit_solution(15800997757416449470)
XLA Ops:
  0.6 64.5 %shard_map.95 = (f32[128,128]{1,0:T(8,128)S(1)}, f32[128,256]{1,0:T(8,128)S(1)}) custom-call(bf16[1,2,64,2048]{3,2,1,0:T(8,128)(2,1)} %root.1, bf16[1,2,192,128]{3,2,1,0:T(8,128)(2,1)} %fc.1, bf16[1,2,192,256]{3,2,1,0:T(8,128)(2,1)} %fg.1, bf16[1,2,2048,128]{3,2,1,0:T(8,128)(2,1)} %dc.1, bf16[1,2,2048,256]{3,2,1,0:T(8,128)(2,1)} %dg.1, s32[2,192]{1,0:T(2,128)} %sc_hbm.1, ...), custom_call_target="tpu_custom_call" | custom-call | flops 3000000000 | bytes 5000000 | tf_op jit(solution)/shard_map/pallas_call | solution.py:752
  65.1 0.6 copy.12
  65.7 0.7 copy.13
